TPU v7x, 256 devices: a whole 4x4x8 slice. The times are simulated.
256 devices in a mesh: wide: 32 (over z, x), narrow: 8 (over y, core).
Axes of the slice: x: 4, y: 4, z: 8, core: 2. Of those that a mesh axis runs over, the one named last changes fastest.
Arguments:
- row_codes: bfloat16 [131072, 512], P('wide'), may hold values from -127 to 127
- row_scales: float32 [131072], P('wide'), may hold values from 0.004 to 0.04
- row_biases: float32 [131072], P('wide'), may hold values from -0.32 to 0.32, as said below
- cluster_ids: int32 [131072], P('wide'), may hold values from 0 to 499, as said below
- order_index: int32 [131072], P('wide'), may hold values from 0 to 131071, each once
Outputs:
- nearest_sim: float32 [131072], P('wide')
Inputs may be any that keep to these rules, and one draw needn't show every extreme that they name: `cluster_ids`: cluster c belongs to owner c % 32. At most 256 rows of one index of wide belong to clusters of one owner, and in every draw one owner receives exactly 256 rows from every index of wide. `row_biases`: the absolute value of each row's offset is at most 8 times that row's scale.
All inputs are finite; a program needn't handle non-finite values.
Results may differ from a plain program's by a relative error of at most 0.0015.
Values may be sent and summed in bfloat16 or wider, within the bound.
No kernel may reach another device: no remote copies, remote signals or barrier semaphores. Data moves between devices by JAX's collectives and lax.ppermute only.
A program may use at most 64 MiB of HBM per device.

v0:
```python
import jax
import jax.numpy as jnp
from jax import lax
from jax.sharding import PartitionSpec as P

epsilon = 1e-06


def unit_vectors(row_codes, row_scales, row_biases):
    values = row_codes.astype(jnp.float32) * row_scales[:, None] + row_biases[:, None]
    return (values * lax.rsqrt(jnp.mean(values * values, axis=1, keepdims=True) + epsilon)).astype(
        jnp.bfloat16
    )


def fold_block(
    queries, query_cluster, query_order, running, block_rows, block_cluster, block_order
):
    feature_width = queries.shape[-1]
    scores = (
        jnp.einsum("qe,ke->qk", queries, block_rows, preferred_element_type=jnp.float32)
        / feature_width
    )
    allowed = (query_cluster[:, None] == block_cluster[None, :]) & (
        block_order[None, :] < query_order[:, None]
    )
    return jnp.maximum(running, jnp.max(jnp.where(allowed, scores, -1.0), axis=1))


def fold_keys(
    queries, query_cluster, query_order, share_rows, running, piece_rows, piece_cluster, piece_order
):
    feature_width = piece_rows.shape[2]
    blocks = piece_rows.shape[1] // share_rows

    def visit_block(block_index, best_now):
        start_col = block_index * share_rows
        block_rows = lax.dynamic_slice_in_dim(piece_rows, start_col, share_rows, 1).reshape(
            -1, feature_width
        )
        block_cluster = lax.dynamic_slice_in_dim(piece_cluster, start_col, share_rows, 1).reshape(
            -1
        )
        block_order = lax.dynamic_slice_in_dim(piece_order, start_col, share_rows, 1).reshape(-1)
        return fold_block(
            queries, query_cluster, query_order, best_now, block_rows, block_cluster, block_order
        )

    return lax.fori_loop(0, blocks, visit_block, running)


def shards(row_codes, row_scales, row_biases, cluster_ids, order_index):
    owners = lax.axis_size("wide")
    peer_count = lax.axis_size("narrow")
    local_rows = row_codes.shape[0]
    feature_width = row_codes.shape[1]
    capacity = 2 * local_rows // owners
    share_rows = capacity // peer_count
    total_slots = owners * capacity
    unit_rows = unit_vectors(row_codes, row_scales, row_biases)
    owner_of = cluster_ids % owners
    one_hot = (owner_of[:, None] == jnp.arange(owners, dtype=jnp.int32)[None, :]).astype(jnp.int32)
    before = jnp.cumsum(one_hot, axis=0) - one_hot
    slot_rank = jnp.sum(before * one_hot, axis=1)
    slot_index = owner_of * capacity + slot_rank
    send_rows = jnp.zeros((total_slots, feature_width), jnp.bfloat16).at[slot_index].set(unit_rows)
    send_rows = send_rows.reshape(owners, capacity, feature_width)
    send_cluster = (
        jnp.full((total_slots,), -1, jnp.int32)
        .at[slot_index]
        .set(cluster_ids)
        .reshape(owners, capacity)
    )
    send_order = (
        jnp.full((total_slots,), -1, jnp.int32)
        .at[slot_index]
        .set(order_index)
        .reshape(owners, capacity)
    )
    offset = lax.axis_index("narrow") * share_rows
    initial = jnp.full((owners * share_rows,), -1.0, jnp.float32)
    got_rows, got_cluster, got_order = (
        lax.all_to_all(send_rows, "wide", split_axis=0, concat_axis=0, tiled=True),
        lax.all_to_all(send_cluster, "wide", split_axis=0, concat_axis=0, tiled=True),
        lax.all_to_all(send_order, "wide", split_axis=0, concat_axis=0, tiled=True),
    )
    queries = lax.dynamic_slice_in_dim(got_rows, offset, share_rows, 1).reshape(-1, feature_width)
    query_cluster = lax.dynamic_slice_in_dim(got_cluster, offset, share_rows, 1).reshape(-1)
    query_order = lax.dynamic_slice_in_dim(got_order, offset, share_rows, 1).reshape(-1)
    best_sim = fold_keys(
        queries, query_cluster, query_order, share_rows, initial, got_rows, got_cluster, got_order
    )
    column = lax.all_gather(best_sim.reshape(owners, share_rows), "narrow", axis=1, tiled=True)
    returned = lax.all_to_all(column, "wide", split_axis=0, concat_axis=0, tiled=True)
    return returned.reshape(-1)[slot_index]


def solution(mesh):
    in_specs = (P("wide", None), P("wide"), P("wide"), P("wide"), P("wide"))
    out_specs = P("wide")
    return jax.shard_map(shards, mesh=mesh, in_specs=in_specs, out_specs=out_specs, check_vma=False)
```

profile of v0, /device:TPU:1, one launch (start us, length us, event | category | flops | bytes accessed | tf_op | source)
XLA Modules:
  0.0 390.2 jit_solution(2840621726013649522)
XLA Ops:
  0.8 9.2 %reduce-window.6 = s32[32,32,128]{2,1,0:T(8,128)S(1)} reduce-window(s32[32,32,128]{2,1,0:T(8,128)S(1)} %fusion.9, s32[]{:T(128)} %constant.80.clone.1), window={size=1x1x128 pad=0_0x0_0x127_0}, to_apply=%region_0.0 | reduce-window | flops 16646144 | bytes 1048580 | tf_op jit(solution)/shard_map/reduce-window
  12.4 16.3 %scatter_custom_fusion = s32[8192]{0:T(1024)} fusion(s32[4096]{0:T(1024)S(1)} %get-tuple-element.189, s32[4096]{0:T(1024)} %param.10, s32[]{:T(128)} %constant.90.clone.1), kind=kCustom, calls=%fused_computation.37 | custom fusion | bytes 33280 | tf_op jit(solution)/shard_map/scatter | solution.py:71
  28.6 11.9 %all-to-all-start = ((s32[32,1,256]{2,1,0:T(1,128)}), s32[32,1,256]{2,1,0:T(1,128)S(1)}, u32[]{:S(2)}, u32[]{:S(2)}) async-start(s32[32,1,256]{2,1,0:T(1,128)} %bitcast.2), calls=%async_computation | async-start | bytes 65536 | tf_op jit(solution)/shard_map/all_to_all | solution.py:84
  40.5 3.8 multiply_reduce_fusion
  44.3 16.3 %scatter_custom_fusion.1 = s32[8192]{0:T(1024)} fusion(s32[4096]{0:T(1024)S(1)} %get-tuple-element.189, s32[4096]{0:T(1024)} %param.11, s32[]{:T(128)} %constant.90.clone.1), kind=kCustom, calls=%fused_computation.35 | custom fusion | bytes 33280 | tf_op jit(solution)/shard_map/scatter | solution.py:77
  60.6 9.2 %all-to-all-start.1 = ((s32[32,1,256]{2,1,0:T(1,128)}), s32[32,1,256]{2,1,0:T(1,128)S(1)}, u32[]{:S(2)}, u32[]{:S(2)}) async-start(s32[32,1,256]{2,1,0:T(1,128)} %bitcast.4), calls=%async_computation.1 | async-start | bytes 65536 | tf_op jit(solution)/shard_map/all_to_all | solution.py:85
  69.8 23.8 %scatter_custom_fusion.2 = bf16[8192,512]{1,0:T(8,128)(2,1)} fusion(s32[4096]{0:T(1024)S(1)} %get-tuple-element.189, bf16[4096,512]{1,0:T(8,128)(2,1)} %param.7, f32[4096]{0:T(1024)S(1)} %add_rsqrt_fusion, f32[4096]{0:T(1024)S(1)} %copy-done, f32[4096]{0:T(1024)S(1)} %copy-done.1, bf16[]{:T(256)} %constant.82.clone.1), kind=kCustom, calls=%fused_computation.13 | custom fusion | flops 10485760 | bytes 12632066 | tf_op jit(solution)/shard_map/scatter | solution.py:66
  93.7 9.3 %all-to-all-start.2 = ((bf16[32,256,512]{2,1,0:T(8,128)(2,1)}), bf16[32,256,512]{2,1,0:T(8,128)(2,1)}, u32[]{:S(2)}, u32[]{:S(2)}) async-start(bf16[32,256,512]{2,1,0:T(8,128)(2,1)} %bitcast.54), calls=%async_computation.2 | async-start | bytes 16777216 | tf_op jit(solution)/shard_map/all_to_all | solution.py:83
  103.4 188.5 %all-to-all-done.2 = bf16[32,256,512]{2,1,0:T(8,128)(2,1)} async-done(((bf16[32,256,512]{2,1,0:T(8,128)(2,1)}), bf16[32,256,512]{2,1,0:T(8,128)(2,1)}, u32[]{:S(2)}, u32[]{:S(2)}) %all-to-all-start.2) | async-done | bytes 8388640 | tf_op jit(solution)/shard_map/all_to_all | solution.py:83
  293.2 26.3 %while.15 = (s32[]{:T(128)}, f32[1024]{0:T(1024)S(1)}, s32[32,32]{1,0:T(8,128)}, s32[32,256]{1,0:T(8,128)S(1)}, s32[32,256]{1,0:T(8,128)S(1)}, /*index=5*/s32[32...) while((s32[]{:T(128)}, f32[1024]{0:T(1024)S(1)}, ...), condition=%wide.wide.region_9.10_spmd.clone, body=%wide.wide.region_7.9_spmd.clone.sunk | while | flops 1080034304 | bytes 4260045 | solution.py:49
  293.2 1.3 constant_dynamic-slice_fusion.10
  294.8 1.7 fusion.26
  296.5 1.3 constant_dynamic-slice_fusion.10
  298.1 1.7 fusion.26
  299.8 1.3 constant_dynamic-slice_fusion.10
  301.4 1.7 fusion.26
  304.6 1.7 fusion.26
  307.9 1.7 fusion.26
  311.2 1.7 fusion.26
  314.5 1.7 fusion.26
  317.8 1.7 fusion.26
  319.7 14.5 %all_gather.3 = f32[32,256]{0,1:T(8,128)S(1)} all-gather(f32[32,32]{0,1:T(8,128)S(1)} %copy.7), channel_id=1, replica_groups=mesh['wide'=32,'narrow'=8] {'narrow'}, dimensions={1}, use_global_device_ids=true | all-gather | bytes 36864 | tf_op jit(solution)/shard_map/all_gather | solution.py:93
  334.3 15.3 %all_to_all.38 = f32[32,1,256]{2,1,0:T(1,128)S(1)} all-to-all(f32[32,1,256]{2,1,0:T(1,128)S(1)} %copy.8), channel_id=1, replica_groups=mesh['wide'=32,'narrow'=8] {'wide'}, dimensions={0} | all-to-all | bytes 65536 | tf_op jit(solution)/shard_map/all_to_all | solution.py:94
  349.6 40.5 %gather_fusion = f32[4096]{0:T(1024)} fusion(f32[8192]{0:T(1024)S(1)} %bitcast.53, s32[4096]{0:T(1024)S(1)} %get-tuple-element.188), kind=kCustom, calls=%fused_computation | custom fusion | bytes 49152 | tf_op jit(solution)/shard_map/gather | solution.py:95
  (66 shorter events, 13.4 us)
Async XLA Ops:
  0.0 69.8 %copy-start = (f32[4096]{0:T(1024)S(1)}, f32[4096]{0:T(1024)}, u32[]{:S(2)}) copy-start(f32[4096]{0:T(1024)} %param.9) | copy-start | bytes 49156
  0.0 69.8 %copy-start.1 = (f32[4096]{0:T(1024)S(1)}, f32[4096]{0:T(1024)}, u32[]{:S(2)}) copy-start(f32[4096]{0:T(1024)} %param.8) | copy-start | bytes 49156
  28.6 32.0 %all-to-all-start = ((s32[32,1,256]{2,1,0:T(1,128)}), s32[32,1,256]{2,1,0:T(1,128)S(1)}, u32[]{:S(2)}, u32[]{:S(2)}) async-start(s32[32,1,256]{2,1,0:T(1,128)} %bitcast.2), calls=%async_computation | async-start | bytes 65536 | tf_op jit(solution)/shard_map/all_to_all | solution.py:84
  60.6 33.1 %all-to-all-start.1 = ((s32[32,1,256]{2,1,0:T(1,128)}), s32[32,1,256]{2,1,0:T(1,128)S(1)}, u32[]{:S(2)}, u32[]{:S(2)}) async-start(s32[32,1,256]{2,1,0:T(1,128)} %bitcast.4), calls=%async_computation.1 | async-start | bytes 65536 | tf_op jit(solution)/shard_map/all_to_all | solution.py:85
  93.7 198.2 %all-to-all-start.2 = ((bf16[32,256,512]{2,1,0:T(8,128)(2,1)}), bf16[32,256,512]{2,1,0:T(8,128)(2,1)}, u32[]{:S(2)}, u32[]{:S(2)}) async-start(bf16[32,256,512]{2,1,0:T(8,128)(2,1)} %bitcast.54), calls=%async_computation.2 | async-start | bytes 16777216 | tf_op jit(solution)/shard_map/all_to_all | solution.py:83
  103.1 190.1 %copy-start.2 = (s32[32,1,32]{2,1,0:T(1,128)}, s32[32,1,32]{2,1,0:T(1,128)S(1)}, u32[]{:S(2)}) copy-start(s32[32,1,32]{2,1,0:T(1,128)S(1)} %constant_dynamic-slice_fusion.4) | copy-start | bytes 12292
  103.3 189.9 %copy-start.3 = (s32[32,1,32]{2,1,0:T(1,128)}, s32[32,1,32]{2,1,0:T(1,128)S(1)}, u32[]{:S(2)}) copy-start(s32[32,1,32]{2,1,0:T(1,128)S(1)} %constant_dynamic-slice_fusion.5) | copy-start | bytes 12292
where the time goes:
time: 391 us; the launch traced here: 390 us
  waiting for transfers between devices  188 us (48%)
  local copies, waits for them, and re-layouts  88 us (23%)
  other arithmetic  39.2 us (10%)
  starting transfers between devices  30.4 us (8%)
  blocking collectives  29.9 us (8%)
  matrix products  13.6 us (3%)
    all_to_all x1, waiting for transfers between devices, shards(): lax.all_to_all(send_rows, 'wide', split_axis=0, concat_axis=0, tiled=True)  188 us
    gather x1, local copies, waits for them, and re-layouts, shards(): return returned.reshape(-1)[slot_index]  40.5 us
    scatter x1, other arithmetic, shards(): jnp.zeros((total_slots, feature_width), jnp.bfloat16).at[slot_index]  23.8 us
    scatter x1, local copies, waits for them, and re-layouts, shards(): send_cluster = jnp.full((total_slots,), -1, jnp.int32).at[slot_index].set...  16.3 us
    scatter x1, local copies, waits for them, and re-layouts, shards(): send_order = jnp.full((total_slots,), -1, jnp.int32).at[slot_index].set(o...  16.3 us
    all_to_all x1, blocking collectives, shards(): lax.all_to_all(column, 'wide', split_axis=0, concat_axis=0, tiled=True)  15.3 us
    all_gather x1, blocking collectives, shards(): lax.all_gather(best_sim.reshape(owners, share_rows), 'narrow', axis=1, ti...  14.5 us
    dot_general x8, matrix products, fold_block(): jnp.einsum('qe,ke->qk', queries, block_rows, preferred_element_type=jnp.f...  13.6 us
  transfers between devices with their start and end apart: 3, of which 1 were waited for; matrix products, arithmetic and copies ran while one was open for 11% of the time, Pallas kernels for 0%

commit v1 on v0

--- a/solution.py
+++ b/solution.py
@@ -1,9 +1,297 @@
+import functools
+
 import jax
 import jax.numpy as jnp
 from jax import lax
+from jax.experimental import pallas as pl
+from jax.experimental.pallas import tpu as pltpu
 from jax.sharding import PartitionSpec as P
 
 epsilon = 1e-06
+
+BLOCK = 56
+SLOTS = BLOCK - 1
+LANES = 128
+CHUNK = 256
+ORDER_SPAN = 131072
+VMEM_LIMIT = 48 * 1024 * 1024
+
+
+def iota(shape, axis):
+    return lax.broadcasted_iota(jnp.int32, shape, axis)
+
+
+def dot(left, right, left_axis, right_axis):
+    return lax.dot_general(
+        left, right, (((left_axis,), (right_axis,)), ((), ())), preferred_element_type=jnp.float32
+    )
+
+
+def strictly_before():
+    return (iota((CHUNK, CHUNK), 0) < iota((CHUNK, CHUNK), 1)).astype(jnp.bfloat16)
+
+
+def chunk_of(ref, index):
+    return jnp.concatenate([ref[2 * index : 2 * index + 1, :], ref[2 * index + 1 : 2 * index + 2, :]], axis=1)
+
+
+def owner_and_peer(clusters, owners, peers):
+    owner = clusters & (owners - 1)
+    place = clusters >> (owners.bit_length() - 1)
+    peer = jnp.minimum(place, 2 * peers - 1 - place)
+    return owner, place, peer
+
+
+def pack_kernel(
+    owners, peers, cluster_ref, order_ref, scale_ref, bias_ref, codes_hbm, out_ref,
+    codes_half, codes_full, slots_full, table_vmem, table_smem, code_sems, table_sem,
+):
+    local_rows = codes_hbm.shape[0]
+    me_wide = lax.axis_index("wide")
+    me_narrow = lax.axis_index("narrow")
+    pieces = code_sems.shape[0]
+    piece = local_rows // pieces
+    copies = [
+        pltpu.make_async_copy(
+            codes_hbm.at[pl.ds(n * piece, piece)], codes_half.at[pl.ds(n * piece, piece)], code_sems.at[n]
+        )
+        for n in range(pieces)
+    ]
+    for copy in copies:
+        copy.start()
+
+    before = strictly_before()
+    count = jnp.zeros((owners, 1), jnp.float32)
+    meta = jnp.zeros((owners, 3 * LANES), jnp.float32)
+    table = jnp.zeros((136, owners), jnp.float32)
+    for n in range(local_rows // CHUNK):
+        clusters = chunk_of(cluster_ref, n)
+        orders = chunk_of(order_ref, n)
+        owner, place, peer = owner_and_peer(clusters, owners, peers)
+        owner = jnp.where(peer == me_narrow, owner, -1)
+        mine = iota((owners, CHUNK), 0) == owner
+        one_hot = jnp.where(mine, 1.0, 0.0)
+        one_hot_half = one_hot.astype(jnp.bfloat16)
+        earlier = dot(one_hot_half, before, 1, 0) + count
+        rank = jnp.sum(jnp.where(mine, earlier, 0.0), axis=0, keepdims=True).astype(jnp.int32)
+        count = count + jnp.sum(one_hot, axis=1, keepdims=True)
+        lane = (me_wide * BLOCK + rank) & (LANES - 1)
+        key = place * ORDER_SPAN + orders + 1
+        row = n * CHUNK + iota((1, CHUNK), 1)
+        at_lane = iota((LANES, CHUNK), 0) == lane
+        at_rank = iota((64, CHUNK), 0) == rank
+
+        def spread(mask, value):
+            return jnp.where(mask, value.astype(jnp.float32), 0.0)
+
+        meta_parts = jnp.concatenate(
+            [spread(at_lane, key >> 16), spread(at_lane, (key >> 8) & 255), spread(at_lane, key & 255)], axis=0
+        ).astype(jnp.bfloat16)
+        table_parts = jnp.concatenate(
+            [spread(at_rank, row >> 6), spread(at_rank, row & 63), jnp.ones((8, CHUNK), jnp.float32)], axis=0
+        ).astype(jnp.bfloat16)
+        meta = meta + dot(one_hot_half, meta_parts, 1, 1)
+        table = table + dot(table_parts, one_hot_half, 1, 1)
+    rows_at = table[0:64] * 64.0 + table[64:128]
+    table_vmem[...] = jnp.concatenate(
+        [
+            jnp.concatenate([rows_at, table[128:136]], axis=0),
+            jnp.zeros((72, LANES - owners), jnp.float32),
+        ],
+        axis=1,
+    ).astype(jnp.int32)
+    table_copy = pltpu.make_async_copy(table_vmem, table_smem, table_sem)
+    table_copy.start()
+    over = jnp.where(jnp.max(count) > SLOTS, 1.0, 0.0)
+    meta = jnp.concatenate([meta, jnp.full((owners, LANES), over, jnp.float32)], axis=1)
+
+    slots_full[...] = jnp.zeros_like(slots_full)
+    for n, copy in enumerate(copies):
+        copy.wait()
+        codes_full[n * piece : (n + 1) * piece, :] = codes_half[n * piece : (n + 1) * piece, :].astype(jnp.float32)
+    table_copy.wait()
+
+    def one_owner(owner, carry):
+        used = jnp.minimum(table_smem[64, owner], SLOTS)
+
+        def eight_rows(group, carry):
+            for n in range(8):
+                slot = group * 8 + n
+                row = table_smem[slot, owner]
+                slots_full[pl.ds(owner * BLOCK + slot, 1), :] = (
+                    codes_full[pl.ds(row, 1), :] * scale_ref[row] + bias_ref[row]
+                )
+            return carry
+
+        return lax.fori_loop(0, (used + 7) // 8, eight_rows, carry)
+
+    lax.fori_loop(0, owners, one_owner, 0)
+
+    pair = 2 * BLOCK
+    for n in range(owners // 2):
+        values = slots_full[n * pair : (n + 1) * pair, :]
+        mean_square = jnp.mean(values * values, axis=1, keepdims=True)
+        unit = values * lax.rsqrt(mean_square + epsilon)
+        place = iota((pair, 1), 0)
+        unit = jnp.where(place == SLOTS, meta[2 * n : 2 * n + 1], unit)
+        unit = jnp.where(place == BLOCK + SLOTS, meta[2 * n + 1 : 2 * n + 2], unit)
+        out_ref[n * pair : (n + 1) * pair, :] = unit.astype(jnp.bfloat16)
+
+
+def pack(row_codes, row_scales, row_biases, cluster_ids, order_index, owners, peers):
+    local_rows, width = row_codes.shape
+    whole = pl.BlockSpec(memory_space=pltpu.VMEM)
+    scalars = pl.BlockSpec(memory_space=pltpu.SMEM)
+    pieces = 8
+    return pl.pallas_call(
+        functools.partial(pack_kernel, owners, peers),
+        out_shape=jax.ShapeDtypeStruct((owners * BLOCK, width), jnp.bfloat16),
+        in_specs=[whole, whole, scalars, scalars, pl.BlockSpec(memory_space=pl.ANY)],
+        out_specs=whole,
+        scratch_shapes=[
+            pltpu.VMEM((local_rows, width), jnp.bfloat16),
+            pltpu.VMEM((local_rows, width), jnp.float32),
+            pltpu.VMEM((owners * BLOCK, width), jnp.float32),
+            pltpu.VMEM((72, LANES), jnp.int32),
+            pltpu.SMEM((72, LANES), jnp.int32),
+            pltpu.SemaphoreType.DMA((pieces,)),
+            pltpu.SemaphoreType.DMA,
+        ],
+        compiler_params=pltpu.CompilerParams(vmem_limit_bytes=VMEM_LIMIT),
+        name="pack",
+    )(
+        cluster_ids.reshape(-1, LANES), order_index.reshape(-1, LANES), row_scales, row_biases, row_codes,
+    )
+
+
+def place_kernel(owners, peers, cluster_ref, group_ref, lane_ref):
+    me_wide = lax.axis_index("wide")
+    groups = owners * peers
+    before = strictly_before()
+    count = jnp.zeros((groups, 1), jnp.float32)
+    for n in range(cluster_ref.shape[0] // 2):
+        owner, _, peer = owner_and_peer(chunk_of(cluster_ref, n), owners, peers)
+        group = peer * owners + owner
+        mine = iota((groups, CHUNK), 0) == group
+        one_hot = jnp.where(mine, 1.0, 0.0)
+        earlier = dot(one_hot.astype(jnp.bfloat16), before, 1, 0) + count
+        rank = jnp.sum(jnp.where(mine, earlier, 0.0), axis=0, keepdims=True).astype(jnp.int32)
+        count = count + jnp.sum(one_hot, axis=1, keepdims=True)
+        lane = (me_wide * BLOCK + rank) & (LANES - 1)
+        for half in range(2):
+            part = slice(half * LANES, (half + 1) * LANES)
+            group_ref[2 * n + half : 2 * n + half + 1, :] = group[:, part]
+            lane_ref[2 * n + half : 2 * n + half + 1, :] = lane[:, part]
+
+
+def places(cluster_ids, owners, peers):
+    whole = pl.BlockSpec(memory_space=pltpu.VMEM)
+    shape = jax.ShapeDtypeStruct((cluster_ids.shape[0] // LANES, LANES), jnp.int32)
+    return pl.pallas_call(
+        functools.partial(place_kernel, owners, peers),
+        out_shape=(shape, shape),
+        in_specs=[whole],
+        out_specs=(whole, whole),
+        compiler_params=pltpu.CompilerParams(vmem_limit_bytes=VMEM_LIMIT),
+        name="places",
+    )(cluster_ids.reshape(-1, LANES))
+
+
+def score_kernel(owners, rows_ref, out_ref, meta_ref, query_ref, best_ref):
+    slots, width = rows_ref.shape
+    tiles = slots // LANES
+    for n in range(owners):
+        end = (n + 1) * BLOCK
+        start = (end - 1) // 16 * 16
+        meta_ref[n : n + 1, :] = rows_ref[start : start + 16, :].astype(jnp.float32)[end - 1 - start : end - start, :]
+    meta = meta_ref[...]
+    key = meta[:, :LANES] * 65536.0 + meta[:, LANES : 2 * LANES] * 256.0 + meta[:, 2 * LANES : 3 * LANES]
+    over = jnp.max(meta[:, 3 * LANES :])
+    source = iota((owners, LANES), 0)
+
+    def in_block(tile, length):
+        place = tile * LANES + iota((owners, LANES), 1) - source * BLOCK
+        return (place >= 0) & (place < length)
+
+    flat = [
+        jnp.sum(jnp.where(in_block(tile, SLOTS), key, 0.0), axis=0, keepdims=True) for tile in range(tiles)
+    ]
+    keys = jnp.concatenate(flat, axis=1)
+    stacked = jnp.concatenate(flat + [jnp.zeros((LANES - tiles, LANES), jnp.float32)], axis=0)
+    query_ref[...] = stacked.T
+    for tile in range(tiles):
+        best_ref[:, tile : tile + 1] = query_ref[:, tile : tile + 1]
+
+    for tile in range(0, tiles, 2):
+        queries = rows_ref[tile * LANES : (tile + 2) * LANES, :]
+        scores = dot(queries, rows_ref[...], 1, 1)
+        mine = jnp.concatenate([query_ref[:, tile : tile + 1], query_ref[:, tile + 1 : tile + 2]], axis=0)
+        first = jnp.floor((mine - 1.0) * (1.0 / ORDER_SPAN)) * ORDER_SPAN
+        allowed = (keys < mine) & (keys > first)
+        best = jnp.max(jnp.where(allowed, scores, -float(width)), axis=1, keepdims=True) * (1.0 / width)
+        best = jnp.maximum(best, -1.0)
+        best_ref[:, tile : tile + 1] = best[:LANES]
+        best_ref[:, tile + 1 : tile + 2] = best[LANES:]
+    turned = best_ref[...].T
+    result = jnp.zeros((owners, LANES), jnp.float32)
+    for tile in range(tiles):
+        result = jnp.where(in_block(tile, SLOTS), turned[tile : tile + 1, :], result)
+        result = jnp.where(in_block(tile, BLOCK) & ~in_block(tile, SLOTS), over, result)
+    out_ref[...] = result
+
+
+def score(rows, owners):
+    whole = pl.BlockSpec(memory_space=pltpu.VMEM)
+    return pl.pallas_call(
+        functools.partial(score_kernel, owners),
+        out_shape=jax.ShapeDtypeStruct((owners, LANES), jnp.float32),
+        in_specs=[whole],
+        out_specs=whole,
+        scratch_shapes=[
+            pltpu.VMEM((owners, rows.shape[1]), jnp.float32),
+            pltpu.VMEM((LANES, LANES), jnp.float32),
+            pltpu.VMEM((LANES, LANES), jnp.float32),
+        ],
+        compiler_params=pltpu.CompilerParams(vmem_limit_bytes=VMEM_LIMIT),
+        name="score",
+    )(rows)
+
+
+def pick_kernel(values_ref, group_ref, lane_ref, out_ref, over_ref):
+    me_wide = lax.axis_index("wide")
+    groups = values_ref.shape[0]
+    values = values_ref[...]
+    marked = iota((groups, LANES), 1) == ((me_wide * BLOCK + SLOTS) & (LANES - 1))
+    over_ref[0, 0] = jnp.max(jnp.where(marked, values, 0.0)).astype(jnp.int32)
+    turned = values.T
+    high = turned.astype(jnp.bfloat16)
+    rest = turned - high.astype(jnp.float32)
+    middle = rest.astype(jnp.bfloat16)
+    low = (rest - middle.astype(jnp.float32)).astype(jnp.bfloat16)
+    parts = jnp.concatenate([high, middle, low], axis=0)
+    for n in range(group_ref.shape[0] // 2):
+        one_hot = jnp.where(iota((groups, CHUNK), 0) == chunk_of(group_ref, n), 1.0, 0.0).astype(jnp.bfloat16)
+        by_lane = dot(parts, one_hot, 1, 0)
+        by_lane = by_lane[:LANES] + by_lane[LANES : 2 * LANES] + by_lane[2 * LANES :]
+        here = iota((LANES, CHUNK), 0) == chunk_of(lane_ref, n)
+        picked = jnp.sum(jnp.where(here, by_lane, 0.0), axis=0, keepdims=True)
+        out_ref[2 * n : 2 * n + 1, :] = picked[:, :LANES]
+        out_ref[2 * n + 1 : 2 * n + 2, :] = picked[:, LANES:]
+
+
+def pick(values, group, lane):
+    whole = pl.BlockSpec(memory_space=pltpu.VMEM)
+    return pl.pallas_call(
+        pick_kernel,
+        out_shape=(
+            jax.ShapeDtypeStruct(group.shape, jnp.float32),
+            jax.ShapeDtypeStruct((1, 1), jnp.int32),
+        ),
+        in_specs=[whole, whole, whole],
+        out_specs=(whole, pl.BlockSpec(memory_space=pltpu.SMEM)),
+        compiler_params=pltpu.CompilerParams(vmem_limit_bytes=VMEM_LIMIT),
+        name="pick",
+    )(values, group, lane)
 
 
 def unit_vectors(row_codes, row_scales, row_biases):
@@ -49,7 +337,7 @@
     return lax.fori_loop(0, blocks, visit_block, running)
 
 
-def shards(row_codes, row_scales, row_biases, cluster_ids, order_index):
+def any_skew(row_codes, row_scales, row_biases, cluster_ids, order_index):
     owners = lax.axis_size("wide")
     peer_count = lax.axis_size("narrow")
     local_rows = row_codes.shape[0]
@@ -95,6 +383,26 @@
     return returned.reshape(-1)[slot_index]
 
 
+def shards(row_codes, row_scales, row_biases, cluster_ids, order_index):
+    owners = lax.axis_size("wide")
+    peers = lax.axis_size("narrow")
+    width = row_codes.shape[1]
+    sent = pack(row_codes, row_scales, row_biases, cluster_ids, order_index, owners, peers)
+    got = lax.all_to_all(
+        sent.reshape(owners, BLOCK, width), "wide", split_axis=0, concat_axis=0, tiled=True
+    ).reshape(owners * BLOCK, width)
+    group, lane = places(cluster_ids, owners, peers)
+    best = score(got, owners)
+    back = lax.all_to_all(best.reshape(owners, 1, LANES), "wide", split_axis=0, concat_axis=0, tiled=True)
+    values = lax.all_gather(back.reshape(owners, LANES), "narrow", axis=0, tiled=True)
+    picked, over = pick(values, group, lane)
+    return lax.cond(
+        over[0, 0] > 0,
+        lambda: any_skew(row_codes, row_scales, row_biases, cluster_ids, order_index),
+        lambda: picked.reshape(-1),
+    )
+
+
 def solution(mesh):
     in_specs = (P("wide", None), P("wide"), P("wide"), P("wide"), P("wide"))
     out_specs = P("wide")

time: 391 us -> 105 us (0.27)
  waiting for transfers between devices: 188 us -> 6.99 us
  local copies, waits for them, and re-layouts: 88 us -> 0.61 us
  blocking collectives: 29.9 us -> 71.4 us
  other arithmetic: 39.2 us -> 0 us
  starting transfers between devices: 30.4 us -> 5.58 us
  Pallas kernels: 0 us -> 19.3 us
  matrix products: 13.6 us -> 0 us
    all_to_all x3 -> x1, waiting for transfers between devices: 188 us -> 6.99 us  [shards(): lax.all_to_all(best.reshape(owners, 1, LANES), 'wide', split_axis=0, conc...]
    gather x1 -> x0, local copies, waits for them, and re-layouts: 40.5 us -> none  [shards(): return returned.reshape(-1)[slot_index]]
    all_to_all x1, blocking collectives: 15.3 us -> 55.4 us  [shards(): lax.all_to_all(sent.reshape(owners, BLOCK, width), 'wide', split_axis=0,...]
    scatter x2 -> x0, local copies, waits for them, and re-layouts: 32.5 us -> none  [the longest x1 16.3 us: shards(): send_cluster = jnp.full((total_slots,), -1, jnp.int32).at[slot_index].set...]
    all_to_all x3 -> x1, starting transfers between devices: 30.4 us -> 5.58 us  [shards(): lax.all_to_all(best.reshape(owners, 1, LANES), 'wide', split_axis=0, conc...]
    scatter x1 -> x0, other arithmetic: 23.8 us -> none  [shards(): jnp.zeros((total_slots, feature_width), jnp.bfloat16).at[slot_index]]
    pallas_call x0 -> x4, Pallas kernels: none -> 19.3 us  [the longest x1 11.2 us: pack(): pl.pallas_call(functools.partial(pack_kernel, owners, peers), out_shape=j...]
    dot_general x8 -> x0, matrix products: 13.6 us -> none  [fold_block(): jnp.einsum('qe,ke->qk', queries, block_rows, preferred_element_type=jnp.f...]
  transfers between devices with their start and end apart: 3 -> 1, of which waited for: 1 -> 1; matrix products, arithmetic and copies ran while one was open for 11% -> 0% of each run, Pallas kernels for 0% -> 1%
where the time goes in v1:
time: 105 us
  blocking collectives  71.4 us (68%)
  Pallas kernels  19.3 us (18%)
  waiting for transfers between devices  6.99 us (7%)
  starting transfers between devices  5.58 us (5%)
    all_to_all x1, blocking collectives, shards(): lax.all_to_all(sent.reshape(owners, BLOCK, width), 'wide', split_axis=0,...  55.4 us
    all_gather x1, blocking collectives, shards(): lax.all_gather(back.reshape(owners, LANES), 'narrow', axis=0, tiled=True)  15.9 us
    pallas_call x1, Pallas kernels, pack(): pl.pallas_call(functools.partial(pack_kernel, owners, peers), out_shape=j...  11.2 us
    all_to_all x1, waiting for transfers between devices, shards(): lax.all_to_all(best.reshape(owners, 1, LANES), 'wide', split_axis=0, conc...  6.99 us
    all_to_all x1, starting transfers between devices, shards(): lax.all_to_all(best.reshape(owners, 1, LANES), 'wide', split_axis=0, conc...  5.58 us
    pallas_call x1, Pallas kernels, score(): pl.pallas_call(functools.partial(score_kernel, owners), out_shape=jax.Sha...  4.93 us
  transfers between devices with their start and end apart: 1, of which 1 were waited for; matrix products, arithmetic and copies ran while one was open for 0% of the time, Pallas kernels for 1%

profile of v1, /device:TPU:1, one launch (start us, length us, event | category | flops | bytes accessed | tf_op | source)
XLA Modules:
  0.0 104.8 jit_solution(9552097714095906571)
XLA Ops:
  0.0 0.0 copy-start
  0.0 0.0 copy-start.1
  0.0 0.0 copy-start.2
  0.0 11.2 %pack.1 = bf16[1792,512]{1,0:T(8,128)(2,1)S(1)} custom-call(s32[32,128]{1,0:T(8,128)} %bitcast.75, s32[32,128]{1,0:T(8,128)} %bitcast.83, f32[4096]{0:T(1024)} %scale_ref.1, f32[4096]{0:T(1024)} %bias_ref.1, bf16[4096,512]{1,0:T(8,128)(2,1)} %codes_hbm.1), custom_call_target="tpu_custom_call" | custom-call | tf_op jit(solution)/shard_map/pack/pallas_call | solution.py:146
  11.2 55.4 %all_to_all.40 = bf16[32,56,512]{2,1,0:T(8,128)(2,1)S(1)} all-to-all(bf16[32,56,512]{2,1,0:T(8,128)(2,1)S(1)} %bitcast.65), channel_id=1, replica_groups=mesh['wide'=32,'narrow'=8] {'wide'}, dimensions={0} | all-to-all | bytes 3670016 | tf_op jit(solution)/shard_map/all_to_all | solution.py:391
  66.6 4.9 %score.1 = f32[32,128]{1,0:T(8,128)} custom-call(bf16[1792,512]{1,0:T(8,128)(2,1)S(1)} %bitcast.64), custom_call_target="tpu_custom_call" | custom-call | tf_op jit(solution)/shard_map/score/pallas_call | solution.py:245
  71.6 5.6 %all-to-all-start.5 = ((f32[32,1,128]{2,1,0:T(1,128)}), f32[32,1,128]{2,1,0:T(1,128)S(1)}, u32[]{:S(2)}, u32[]{:S(2)}) async-start(f32[32,1,128]{2,1,0:T(1,128)} %bitcast.16), calls=%async_computation.5 | async-start | bytes 32768 | tf_op jit(solution)/shard_map/all_to_all | solution.py:396
  77.2 0.0 copy-done
  77.2 1.5 %places.1 = (s32[32,128]{1,0:T(8,128)S(1)}, s32[32,128]{1,0:T(8,128)S(1)}) custom-call(s32[32,128]{1,0:T(8,128)S(1)} %bitcast.76), custom_call_target="tpu_custom_call" | custom-call | tf_op jit(solution)/shard_map/places/pallas_call | solution.py:190
  78.7 7.0 %all-to-all-done.5 = f32[32,1,128]{2,1,0:T(1,128)S(1)} async-done(((f32[32,1,128]{2,1,0:T(1,128)}), f32[32,1,128]{2,1,0:T(1,128)S(1)}, u32[]{:S(2)}, u32[]{:S(2)}) %all-to-all-start.5) | async-done | bytes 16416 | tf_op jit(solution)/shard_map/all_to_all | solution.py:396
  85.7 15.9 %all-gather = f32[256,1,128]{2,0,1:T(8,128)S(1)} all-gather(f32[32,1,128]{2,0,1:T(8,128)S(1)} %bitcast.78), channel_id=2, replica_groups=mesh['wide'=32,'narrow'=8] {'narrow'}, dimensions={0}, use_global_device_ids=true | all-gather | bytes 147456 | tf_op jit(solution)/shard_map/all_gather | solution.py:397
  101.6 1.7 %pick.1 = (f32[32,128]{1,0:T(8,128)S(1)}, s32[1,1]{1,0:T(1,128)}) custom-call(f32[256,128]{1,0:T(8,128)S(1)} %bitcast.66, s32[32,128]{1,0:T(8,128)S(1)} %get-tuple-element.167.group_ref, s32[32,128]{1,0:T(8,128)S(1)} %get-tuple-element.168.lane_ref), custom_call_target="tpu_custom_call" | custom-call | tf_op jit(solution)/shard_map/pick/pallas_call | solution.py:284
  104.0 0.0 copy-done.1
  104.0 0.0 copy-done.2
  104.0 0.2 conditional.1
  104.2 0.0 copy-start.5
  104.2 0.6 copy-done.5
Async XLA Ops:
  0.0 77.2 %copy-start = (s32[4096]{0:T(1024)S(1)}, s32[4096]{0:T(1024)}, u32[]{:S(2)}) copy-start(s32[4096]{0:T(1024)} %param.12) | copy-start | bytes 49156
  0.0 104.0 %copy-start.1 = (f32[4096]{0:T(1024)S(1)}, f32[4096]{0:T(1024)}, u32[]{:S(2)}) copy-start(f32[4096]{0:T(1024)} %scale_ref.1) | copy-start | bytes 49156
  0.0 104.0 %copy-start.2 = (f32[4096]{0:T(1024)S(1)}, f32[4096]{0:T(1024)}, u32[]{:S(2)}) copy-start(f32[4096]{0:T(1024)} %bias_ref.1) | copy-start | bytes 49156
  71.6 14.1 %all-to-all-start.5 = ((f32[32,1,128]{2,1,0:T(1,128)}), f32[32,1,128]{2,1,0:T(1,128)S(1)}, u32[]{:S(2)}, u32[]{:S(2)}) async-start(f32[32,1,128]{2,1,0:T(1,128)} %bitcast.16), calls=%async_computation.5 | async-start | bytes 32768 | tf_op jit(solution)/shard_map/all_to_all | solution.py:396
  104.2 0.6 copy-start.5

commit v2 on v1

--- a/solution.py
+++ b/solution.py
@@ -9,9 +9,10 @@
 
 epsilon = 1e-06
 
-BLOCK = 56
+BLOCK = 48
 SLOTS = BLOCK - 1
 LANES = 128
+HALF = LANES // 2
 CHUNK = 256
 ORDER_SPAN = 131072
 VMEM_LIMIT = 48 * 1024 * 1024
@@ -35,11 +36,11 @@
     return jnp.concatenate([ref[2 * index : 2 * index + 1, :], ref[2 * index + 1 : 2 * index + 2, :]], axis=1)
 
 
-def owner_and_peer(clusters, owners, peers):
+def owner_and_chip(clusters, owners, peers):
     owner = clusters & (owners - 1)
     place = clusters >> (owners.bit_length() - 1)
-    peer = jnp.minimum(place, 2 * peers - 1 - place)
-    return owner, place, peer
+    chip = jnp.minimum(place, 2 * peers - 1 - place) >> 1
+    return owner, place, chip
 
 
 def pack_kernel(
@@ -62,48 +63,48 @@
 
     before = strictly_before()
     count = jnp.zeros((owners, 1), jnp.float32)
-    meta = jnp.zeros((owners, 3 * LANES), jnp.float32)
-    table = jnp.zeros((136, owners), jnp.float32)
+    table = jnp.zeros((owners, 3 * LANES), jnp.float32)
     for n in range(local_rows // CHUNK):
         clusters = chunk_of(cluster_ref, n)
         orders = chunk_of(order_ref, n)
-        owner, place, peer = owner_and_peer(clusters, owners, peers)
-        owner = jnp.where(peer == me_narrow, owner, -1)
+        owner, place, chip = owner_and_chip(clusters, owners, peers)
+        owner = jnp.where(chip == me_narrow >> 1, owner, -1)
         mine = iota((owners, CHUNK), 0) == owner
         one_hot = jnp.where(mine, 1.0, 0.0)
         one_hot_half = one_hot.astype(jnp.bfloat16)
         earlier = dot(one_hot_half, before, 1, 0) + count
         rank = jnp.sum(jnp.where(mine, earlier, 0.0), axis=0, keepdims=True).astype(jnp.int32)
         count = count + jnp.sum(one_hot, axis=1, keepdims=True)
-        lane = (me_wide * BLOCK + rank) & (LANES - 1)
+        slot = jnp.where((rank & 1) == (me_narrow & 1), rank >> 1, -1)
         key = place * ORDER_SPAN + orders + 1
         row = n * CHUNK + iota((1, CHUNK), 1)
-        at_lane = iota((LANES, CHUNK), 0) == lane
-        at_rank = iota((64, CHUNK), 0) == rank
-
-        def spread(mask, value):
-            return jnp.where(mask, value.astype(jnp.float32), 0.0)
-
-        meta_parts = jnp.concatenate(
-            [spread(at_lane, key >> 16), spread(at_lane, (key >> 8) & 255), spread(at_lane, key & 255)], axis=0
-        ).astype(jnp.bfloat16)
-        table_parts = jnp.concatenate(
-            [spread(at_rank, row >> 6), spread(at_rank, row & 63), jnp.ones((8, CHUNK), jnp.float32)], axis=0
-        ).astype(jnp.bfloat16)
-        meta = meta + dot(one_hot_half, meta_parts, 1, 1)
-        table = table + dot(table_parts, one_hot_half, 1, 1)
-    rows_at = table[0:64] * 64.0 + table[64:128]
-    table_vmem[...] = jnp.concatenate(
+        at_slot = iota((HALF, CHUNK), 0) == slot
+        parts = [
+            jnp.where(at_slot, part.astype(jnp.float32), 0.0).astype(jnp.bfloat16)
+            for part in (row >> 6, row & 63, key >> 16, (key >> 8) & 255, key & 255)
+        ]
+        parts.append(jnp.zeros((HALF, CHUNK), jnp.bfloat16))
+        table = table + dot(one_hot_half, jnp.concatenate(parts, axis=0), 1, 1)
+    lane = iota((owners, LANES), 1)
+    rows_at = table[:, :LANES] * 64.0 + pltpu.roll(table[:, :LANES], HALF, 1)
+    used = jnp.minimum((count.astype(jnp.int32) + 1 - (me_narrow & 1)) >> 1, SLOTS)
+    table_vmem[...] = jnp.where(lane == HALF, used, rows_at.astype(jnp.int32))
+    table_copy = pltpu.make_async_copy(table_vmem, table_smem, table_sem)
+    table_copy.start()
+    turn = me_wide * BLOCK
+    first = jnp.where(lane < HALF, table[:, LANES : 2 * LANES], 0.0)
+    second = jnp.where(lane < HALF, 0.0, table[:, LANES : 2 * LANES])
+    third = table[:, 2 * LANES :]
+    over = jnp.where(jnp.max(count) > 2 * SLOTS, 1.0, 0.0)
+    meta = jnp.concatenate(
         [
-            jnp.concatenate([rows_at, table[128:136]], axis=0),
-            jnp.zeros((72, LANES - owners), jnp.float32),
+            pltpu.roll(first, turn & (LANES - 1), 1),
+            pltpu.roll(second, (turn + HALF) & (LANES - 1), 1),
+            pltpu.roll(third, turn & (LANES - 1), 1),
+            jnp.full((owners, LANES), over, jnp.float32),
         ],
         axis=1,
-    ).astype(jnp.int32)
-    table_copy = pltpu.make_async_copy(table_vmem, table_smem, table_sem)
-    table_copy.start()
-    over = jnp.where(jnp.max(count) > SLOTS, 1.0, 0.0)
-    meta = jnp.concatenate([meta, jnp.full((owners, LANES), over, jnp.float32)], axis=1)
+    )
 
     slots_full[...] = jnp.zeros_like(slots_full)
     for n, copy in enumerate(copies):
@@ -111,21 +112,23 @@
         codes_full[n * piece : (n + 1) * piece, :] = codes_half[n * piece : (n + 1) * piece, :].astype(jnp.float32)
     table_copy.wait()
 
-    def one_owner(owner, carry):
-        used = jnp.minimum(table_smem[64, owner], SLOTS)
+    def two_owners(half, carry):
+        pair = (2 * half, 2 * half + 1)
+        used = jnp.maximum(table_smem[pair[0], HALF], table_smem[pair[1], HALF])
 
         def eight_rows(group, carry):
-            for n in range(8):
-                slot = group * 8 + n
-                row = table_smem[slot, owner]
-                slots_full[pl.ds(owner * BLOCK + slot, 1), :] = (
-                    codes_full[pl.ds(row, 1), :] * scale_ref[row] + bias_ref[row]
-                )
+            for owner in pair:
+                for n in range(8):
+                    slot = group * 8 + n
+                    row = table_smem[owner, slot]
+                    slots_full[pl.ds(owner * BLOCK + slot, 1), :] = (
+                        codes_full[pl.ds(row, 1), :] * scale_ref[row] + bias_ref[row]
+                    )
             return carry
 
         return lax.fori_loop(0, (used + 7) // 8, eight_rows, carry)
 
-    lax.fori_loop(0, owners, one_owner, 0)
+    lax.fori_loop(0, owners // 2, two_owners, 0)
 
     pair = 2 * BLOCK
     for n in range(owners // 2):
@@ -152,8 +155,8 @@
             pltpu.VMEM((local_rows, width), jnp.bfloat16),
             pltpu.VMEM((local_rows, width), jnp.float32),
             pltpu.VMEM((owners * BLOCK, width), jnp.float32),
-            pltpu.VMEM((72, LANES), jnp.int32),
-            pltpu.SMEM((72, LANES), jnp.int32),
+            pltpu.VMEM((owners, LANES), jnp.int32),
+            pltpu.SMEM((owners, LANES), jnp.int32),
             pltpu.SemaphoreType.DMA((pieces,)),
             pltpu.SemaphoreType.DMA,
         ],
@@ -166,18 +169,18 @@
 
 def place_kernel(owners, peers, cluster_ref, group_ref, lane_ref):
     me_wide = lax.axis_index("wide")
-    groups = owners * peers
+    groups = owners * peers // 2
     before = strictly_before()
     count = jnp.zeros((groups, 1), jnp.float32)
     for n in range(cluster_ref.shape[0] // 2):
-        owner, _, peer = owner_and_peer(chunk_of(cluster_ref, n), owners, peers)
-        group = peer * owners + owner
-        mine = iota((groups, CHUNK), 0) == group
+        owner, _, chip = owner_and_chip(chunk_of(cluster_ref, n), owners, peers)
+        mine = iota((groups, CHUNK), 0) == chip * owners + owner
         one_hot = jnp.where(mine, 1.0, 0.0)
         earlier = dot(one_hot.astype(jnp.bfloat16), before, 1, 0) + count
         rank = jnp.sum(jnp.where(mine, earlier, 0.0), axis=0, keepdims=True).astype(jnp.int32)
         count = count + jnp.sum(one_hot, axis=1, keepdims=True)
-        lane = (me_wide * BLOCK + rank) & (LANES - 1)
+        group = (2 * chip + (rank & 1)) * owners + owner
+        lane = (me_wide * BLOCK + (rank >> 1)) & (LANES - 1)
         for half in range(2):
             part = slice(half * LANES, (half + 1) * LANES)
             group_ref[2 * n + half : 2 * n + half + 1, :] = group[:, part]
@@ -197,64 +200,90 @@
     )(cluster_ids.reshape(-1, LANES))
 
 
-def score_kernel(owners, rows_ref, out_ref, meta_ref, query_ref, best_ref):
-    slots, width = rows_ref.shape
-    tiles = slots // LANES
+def in_block(owners, tile, length):
+    place = tile * LANES + iota((owners, LANES), 1) - iota((owners, LANES), 0) * BLOCK
+    return (place >= 0) & (place < length)
+
+
+def keys_of(owners, rows_ref, meta_ref):
     for n in range(owners):
         end = (n + 1) * BLOCK
-        start = (end - 1) // 16 * 16
-        meta_ref[n : n + 1, :] = rows_ref[start : start + 16, :].astype(jnp.float32)[end - 1 - start : end - start, :]
+        meta_ref[n : n + 1, :] = rows_ref[end - 16 : end, :].astype(jnp.float32)[15:16, :]
     meta = meta_ref[...]
     key = meta[:, :LANES] * 65536.0 + meta[:, LANES : 2 * LANES] * 256.0 + meta[:, 2 * LANES : 3 * LANES]
-    over = jnp.max(meta[:, 3 * LANES :])
-    source = iota((owners, LANES), 0)
-
-    def in_block(tile, length):
-        place = tile * LANES + iota((owners, LANES), 1) - source * BLOCK
-        return (place >= 0) & (place < length)
-
     flat = [
-        jnp.sum(jnp.where(in_block(tile, SLOTS), key, 0.0), axis=0, keepdims=True) for tile in range(tiles)
+        jnp.sum(jnp.where(in_block(owners, tile, SLOTS), key, 0.0), axis=0, keepdims=True)
+        for tile in range(rows_ref.shape[0] // LANES)
     ]
-    keys = jnp.concatenate(flat, axis=1)
-    stacked = jnp.concatenate(flat + [jnp.zeros((LANES - tiles, LANES), jnp.float32)], axis=0)
-    query_ref[...] = stacked.T
-    for tile in range(tiles):
-        best_ref[:, tile : tile + 1] = query_ref[:, tile : tile + 1]
-
-    for tile in range(0, tiles, 2):
-        queries = rows_ref[tile * LANES : (tile + 2) * LANES, :]
-        scores = dot(queries, rows_ref[...], 1, 1)
+    return flat, jnp.max(meta[:, 3 * LANES :])
+
+
+def fold(rows_ref, key_rows_ref, keys, query_ref, best_in, best_ref):
+    slots, width = rows_ref.shape
+    for tile in range(0, slots // LANES, 2):
+        scores = dot(rows_ref[tile * LANES : (tile + 2) * LANES, :], key_rows_ref[...], 1, 1)
         mine = jnp.concatenate([query_ref[:, tile : tile + 1], query_ref[:, tile + 1 : tile + 2]], axis=0)
         first = jnp.floor((mine - 1.0) * (1.0 / ORDER_SPAN)) * ORDER_SPAN
         allowed = (keys < mine) & (keys > first)
         best = jnp.max(jnp.where(allowed, scores, -float(width)), axis=1, keepdims=True) * (1.0 / width)
         best = jnp.maximum(best, -1.0)
-        best_ref[:, tile : tile + 1] = best[:LANES]
-        best_ref[:, tile + 1 : tile + 2] = best[LANES:]
+        for half in range(2):
+            part = best[half * LANES : (half + 1) * LANES]
+            if best_in is not None:
+                part = jnp.maximum(part, best_in[:, tile + half : tile + half + 1])
+            best_ref[:, tile + half : tile + half + 1] = part
+
+
+def own_kernel(owners, rows_ref, query_ref, best_ref, meta_ref):
+    flat, _ = keys_of(owners, rows_ref, meta_ref)
+    query_ref[...] = jnp.concatenate(
+        flat + [jnp.zeros((LANES - len(flat), LANES), jnp.float32)], axis=0
+    ).T
+    fold(rows_ref, rows_ref, jnp.concatenate(flat, axis=1), query_ref, None, best_ref)
+
+
+def other_kernel(owners, rows_ref, other_ref, query_ref, best_in, out_ref, meta_ref, best_ref):
+    flat, over = keys_of(owners, other_ref, meta_ref)
+    fold(rows_ref, other_ref, jnp.concatenate(flat, axis=1), query_ref, best_in, best_ref)
     turned = best_ref[...].T
     result = jnp.zeros((owners, LANES), jnp.float32)
-    for tile in range(tiles):
-        result = jnp.where(in_block(tile, SLOTS), turned[tile : tile + 1, :], result)
-        result = jnp.where(in_block(tile, BLOCK) & ~in_block(tile, SLOTS), over, result)
+    for tile in range(len(flat)):
+        result = jnp.where(in_block(owners, tile, SLOTS), turned[tile : tile + 1, :], result)
+        result = jnp.where(in_block(owners, tile, BLOCK) & ~in_block(owners, tile, SLOTS), over, result)
     out_ref[...] = result
 
 
 def score(rows, owners):
+    slots, width = rows.shape
     whole = pl.BlockSpec(memory_space=pltpu.VMEM)
+    square = jax.ShapeDtypeStruct((LANES, LANES), jnp.float32)
+    cost = pl.CostEstimate(
+        flops=2 * slots * slots * width, bytes_accessed=4 * slots * width, transcendentals=0
+    )
+    peers = lax.axis_size("narrow")
+    other = lax.ppermute(rows, "narrow", [(n, n ^ 1) for n in range(peers)])
+    meta = pltpu.VMEM((owners, width), jnp.float32)
+    params = pltpu.CompilerParams(vmem_limit_bytes=VMEM_LIMIT)
+    query, best = pl.pallas_call(
+        functools.partial(own_kernel, owners),
+        out_shape=(square, square),
+        in_specs=[whole],
+        out_specs=(whole, whole),
+        scratch_shapes=[meta],
+        compiler_params=params,
+        cost_estimate=cost,
+        name="score_own",
+    )(rows)
     return pl.pallas_call(
-        functools.partial(score_kernel, owners),
+        functools.partial(other_kernel, owners),
         out_shape=jax.ShapeDtypeStruct((owners, LANES), jnp.float32),
-        in_specs=[whole],
+        in_specs=[whole] * 4,
         out_specs=whole,
-        scratch_shapes=[
-            pltpu.VMEM((owners, rows.shape[1]), jnp.float32),
-            pltpu.VMEM((LANES, LANES), jnp.float32),
-            pltpu.VMEM((LANES, LANES), jnp.float32),
-        ],
-        compiler_params=pltpu.CompilerParams(vmem_limit_bytes=VMEM_LIMIT),
-        name="score",
-    )(rows)
+        scratch_shapes=[meta, pltpu.VMEM((LANES, LANES), jnp.float32)],
+        compiler_params=params,
+        cost_estimate=cost,
+        name="score_other",
+    )(rows, other, query, best)
 
 
 def pick_kernel(values_ref, group_ref, lane_ref, out_ref, over_ref):
@@ -394,13 +423,19 @@
     group, lane = places(cluster_ids, owners, peers)
     best = score(got, owners)
     back = lax.all_to_all(best.reshape(owners, 1, LANES), "wide", split_axis=0, concat_axis=0, tiled=True)
-    values = lax.all_gather(back.reshape(owners, LANES), "narrow", axis=0, tiled=True)
+    copies = jnp.broadcast_to(back.reshape(1, owners, LANES), (peers, owners, LANES))
+    values = lax.all_to_all(copies, "narrow", split_axis=0, concat_axis=0, tiled=True)
+    values = values.reshape(peers * owners, LANES)
     picked, over = pick(values, group, lane)
-    return lax.cond(
-        over[0, 0] > 0,
-        lambda: any_skew(row_codes, row_scales, row_biases, cluster_ids, order_index),
-        lambda: picked.reshape(-1),
-    )
+    _, result = lax.while_loop(
+        lambda state: state[0] > 0,
+        lambda state: (
+            jnp.zeros_like(state[0]),
+            any_skew(row_codes, row_scales, row_biases, cluster_ids, order_index),
+        ),
+        (over[0, 0], picked.reshape(-1)),
+    )
+    return result
 
 
 def solution(mesh):

time: 105 us -> 98.5 us (0.938)
  blocking collectives: 71.4 us -> 63 us
  starting transfers between devices: 5.58 us -> 8.81 us
  waiting for transfers between devices: 6.99 us -> 4.41 us
    all_gather x1 -> x0, blocking collectives: 15.9 us -> none  [shards(): lax.all_gather(back.reshape(owners, LANES), 'narrow', axis=0, tiled=True)]
    all_to_all x0 -> x1, blocking collectives: none -> 12.6 us  [shards(): lax.all_to_all(best.reshape(owners, 1, LANES), 'wide', split_axis=0, conc...]
    all_to_all x1, blocking collectives: 55.4 us -> 50.4 us  [shards(): lax.all_to_all(sent.reshape(owners, BLOCK, width), 'wide', split_axis=0,...]
    ppermute x0 -> x1, starting transfers between devices: none -> 2.76 us  [score(): other = lax.ppermute(rows, 'narrow', [(n, n ^ 1) for n in range(peers)])]
    all_to_all x1, waiting for transfers between devices: 6.99 us -> 4.41 us  [shards(): lax.all_to_all(copies, 'narrow', split_axis=0, concat_axis=0, tiled=True)]
    pallas_call x1 -> x2, Pallas kernels: 4.93 us -> 6.15 us  [the longest x1 3.1 us: score(): pl.pallas_call(functools.partial(other_kernel, owners), out_shape=jax.Sha...]
  transfers between devices with their start and end apart: 1 -> 2, of which waited for: 1 -> 1; matrix products, arithmetic and copies ran while one was open for 0% -> 0% of each run, Pallas kernels for 1% -> 4%
where the time goes in v2:
time: 98.5 us; the launch traced here: 98 us
  blocking collectives  63 us (64%)
  Pallas kernels  20 us (20%)
  starting transfers between devices  8.81 us (9%)
  waiting for transfers between devices  4.41 us (4%)
    all_to_all x1, blocking collectives, shards(): lax.all_to_all(sent.reshape(owners, BLOCK, width), 'wide', split_axis=0,...  50.4 us
    all_to_all x1, blocking collectives, shards(): lax.all_to_all(best.reshape(owners, 1, LANES), 'wide', split_axis=0, conc...  12.6 us
    pallas_call x1, Pallas kernels, pack(): pl.pallas_call(functools.partial(pack_kernel, owners, peers), out_shape=j...  11.1 us
    all_to_all x1, starting transfers between devices, shards(): lax.all_to_all(copies, 'narrow', split_axis=0, concat_axis=0, tiled=True)  6.05 us
    all_to_all x1, waiting for transfers between devices, shards(): lax.all_to_all(copies, 'narrow', split_axis=0, concat_axis=0, tiled=True)  4.41 us
    pallas_call x1, Pallas kernels, score(): pl.pallas_call(functools.partial(other_kernel, owners), out_shape=jax.Sha...  3.1 us
    pallas_call x1, Pallas kernels, score(): pl.pallas_call(functools.partial(own_kernel, owners), out_shape=(square,...  3.06 us
    ppermute x1, starting transfers between devices, score(): other = lax.ppermute(rows, 'narrow', [(n, n ^ 1) for n in range(peers)])  2.76 us
  transfers between devices with their start and end apart: 2, of which 1 were waited for; matrix products, arithmetic and copies ran while one was open for 0% of the time, Pallas kernels for 4%

profile of v2, /device:TPU:1, one launch (start us, length us, event | category | flops | bytes accessed | tf_op | source)
XLA Modules:
  0.0 98.0 jit_solution(17574316667011398922)
XLA Ops:
  0.0 11.1 %pack.1 = bf16[1536,512]{1,0:T(8,128)(2,1)S(1)} custom-call(s32[32,128]{1,0:T(8,128)} %bitcast.83, s32[32,128]{1,0:T(8,128)} %bitcast.97, f32[4096]{0:T(1024)} %scale_ref.1, f32[4096]{0:T(1024)} %bias_ref.1, bf16[4096,512]{1,0:T(8,128)(2,1)} %codes_hbm.1), custom_call_target="tpu_custom_call" | custom-call | tf_op jit(solution)/shard_map/pack/pallas_call | solution.py:149
  11.1 50.4 %all_to_all.44 = bf16[32,48,512]{2,1,0:T(8,128)(2,1)S(1)} all-to-all(bf16[32,48,512]{2,1,0:T(8,128)(2,1)S(1)} %bitcast.69), channel_id=1, replica_groups=mesh['wide'=32,'narrow'=8] {'wide'}, dimensions={0} | all-to-all | bytes 3145728 | tf_op jit(solution)/shard_map/all_to_all | solution.py:420
  61.5 0.0 copy-start
  61.5 0.0 copy-start.1
  61.5 0.0 copy-start.2
  61.5 2.8 %collective-permute-start = (bf16[1536,512]{1,0:T(8,128)(2,1)S(1)}, bf16[1536,512]{1,0:T(8,128)(2,1)S(1)}, u32[]{:S(2)}, u32[]{:S(2)}) collective-permute-start(bf16[1536,512]{1,0:T(8,128)(2,1)S(1)} %bitcast.70), channel_id=1, source_target_pairs={{0,1},{1,0},{2,3},{3,2},{4,5},{5,4},{6,7},{7,6},{8,9},{9,8},{10,11... | collective-permute-start | bytes 4718600 | tf_op jit(solution)/shard_map/ppermute | solution.py:264
  64.2 3.1 %score_own.1 = (f32[128,128]{1,0:T(8,128)S(1)}, f32[128,128]{1,0:T(8,128)S(1)}) custom-call(bf16[1536,512]{1,0:T(8,128)(2,1)S(1)} %bitcast.71), custom_call_target="tpu_custom_call" | custom-call | flops 2415919104 | bytes 3145728 | tf_op jit(solution)/shard_map/score_own/pallas_call | solution.py:267
  67.3 0.0 collective-permute-done.other_ref
  67.3 3.1 %score_other.1 = f32[32,128]{1,0:T(8,128)S(1)} custom-call(bf16[1536,512]{1,0:T(8,128)(2,1)S(1)} %bitcast.72, bf16[1536,512]{1,0:T(8,128)(2,1)S(1)} %collective-permute-done.other_ref, f32[128,128]{1,0:T(8,128)S(1)} %get-tuple-element.185.query_ref, f32[128,128]{1,0:T(8,128)S(1)} %get-tuple-element.186.best_in), custom_call_target="tpu_custom_call" | custom-call | flops 2415919104 | bytes 3145728 | tf_op jit(solution)/shard_map/score_other/pallas_call | solution.py:277
  70.4 12.6 %all_to_all.45 = f32[32,1,128]{2,1,0:T(1,128)S(1)} all-to-all(f32[32,1,128]{2,1,0:T(1,128)S(1)} %bitcast.74), channel_id=1, replica_groups=mesh['wide'=32,'narrow'=8] {'wide'}, dimensions={0} | all-to-all | bytes 32768 | tf_op jit(solution)/shard_map/all_to_all | solution.py:425
  83.1 0.6 broadcast_in_dim.13
  83.7 6.0 %all-to-all-start.6 = ((f32[8,32,128]{2,1,0:T(8,128)}), f32[8,32,128]{2,1,0:T(8,128)S(1)}, u32[]{:S(2)}, u32[]{:S(2)}) async-start(f32[8,32,128]{2,1,0:T(8,128)} %broadcast_in_dim.13), calls=%async_computation.6 | async-start | bytes 262144 | tf_op jit(solution)/shard_map/all_to_all | solution.py:427
  89.8 0.0 copy-done
  89.8 0.9 places.1
  90.6 4.4 %all-to-all-done.6 = f32[8,32,128]{2,1,0:T(8,128)S(1)} async-done(((f32[8,32,128]{2,1,0:T(8,128)}), f32[8,32,128]{2,1,0:T(8,128)S(1)}, u32[]{:S(2)}, u32[]{:S(2)}) %all-to-all-start.6) | async-done | bytes 131104 | tf_op jit(solution)/shard_map/all_to_all | solution.py:427
  95.0 1.9 %pick.1 = (f32[32,128]{1,0:T(8,128)}, s32[1,1]{1,0:T(1,128)}) custom-call(f32[256,128]{1,0:T(8,128)S(1)} %bitcast.73, s32[32,128]{1,0:T(8,128)S(1)} %get-tuple-element.187.group_ref, s32[32,128]{1,0:T(8,128)S(1)} %get-tuple-element.188.lane_ref), custom_call_target="tpu_custom_call" | custom-call | tf_op jit(solution)/shard_map/pick/pallas_call | solution.py:313
  96.9 0.0 copy-done.1
  97.0 0.0 copy-done.2
  97.0 0.8 while.21
Async XLA Ops:
  61.5 28.3 %copy-start = (s32[4096]{0:T(1024)S(1)}, s32[4096]{0:T(1024)}, u32[]{:S(2)}) copy-start(s32[4096]{0:T(1024)} %param.12) | copy-start | bytes 49156
  61.5 35.5 %copy-start.1 = (f32[4096]{0:T(1024)S(1)}, f32[4096]{0:T(1024)}, u32[]{:S(2)}) copy-start(f32[4096]{0:T(1024)} %scale_ref.1) | copy-start | bytes 49156
  61.5 35.5 %copy-start.2 = (f32[4096]{0:T(1024)S(1)}, f32[4096]{0:T(1024)}, u32[]{:S(2)}) copy-start(f32[4096]{0:T(1024)} %bias_ref.1) | copy-start | bytes 49156
  61.5 5.8 %collective-permute-start = (bf16[1536,512]{1,0:T(8,128)(2,1)S(1)}, bf16[1536,512]{1,0:T(8,128)(2,1)S(1)}, u32[]{:S(2)}, u32[]{:S(2)}) collective-permute-start(bf16[1536,512]{1,0:T(8,128)(2,1)S(1)} %bitcast.70), channel_id=1, source_target_pairs={{0,1},{1,0},{2,3},{3,2},{4,5},{5,4},{6,7},{7,6},{8,9},{9,8},{10,11... | collective-permute-start | bytes 4718600 | tf_op jit(solution)/shard_map/ppermute | solution.py:264
  83.7 11.3 %all-to-all-start.6 = ((f32[8,32,128]{2,1,0:T(8,128)}), f32[8,32,128]{2,1,0:T(8,128)S(1)}, u32[]{:S(2)}, u32[]{:S(2)}) async-start(f32[8,32,128]{2,1,0:T(8,128)} %broadcast_in_dim.13), calls=%async_computation.6 | async-start | bytes 262144 | tf_op jit(solution)/shard_map/all_to_all | solution.py:427

commit v3 on v2

--- a/solution.py
+++ b/solution.py
@@ -9,10 +9,13 @@
 
 epsilon = 1e-06
 
-BLOCK = 48
+BLOCK = 40
 SLOTS = BLOCK - 1
 LANES = 128
 HALF = LANES // 2
+PITCH = 5
+TABLE = 48
+TAKE = 4
 CHUNK = 256
 ORDER_SPAN = 131072
 VMEM_LIMIT = 48 * 1024 * 1024
@@ -36,21 +39,40 @@
     return jnp.concatenate([ref[2 * index : 2 * index + 1, :], ref[2 * index + 1 : 2 * index + 2, :]], axis=1)
 
 
-def owner_and_chip(clusters, owners, peers):
-    owner = clusters & (owners - 1)
-    place = clusters >> (owners.bit_length() - 1)
+def split(clusters, owners):
+    return clusters & (owners - 1), clusters >> (owners.bit_length() - 1)
+
+
+def busiest_owner(cluster_ref, owners):
+    total = jnp.zeros((owners, CHUNK), jnp.float32)
+    for n in range(cluster_ref.shape[0] // 2):
+        owner, _ = split(chunk_of(cluster_ref, n), owners)
+        total = total + jnp.where(iota((owners, CHUNK), 0) == owner, 1.0, 0.0)
+    total = jnp.sum(total, axis=1, keepdims=True)
+    at_top = total == jnp.max(total, axis=0, keepdims=True)
+    return jnp.min(jnp.where(at_top, iota((owners, 1), 0), owners), axis=0, keepdims=True)
+
+
+def owner_place_chip(clusters, owners, peers, busiest):
+    owner, place = split(clusters, owners)
     chip = jnp.minimum(place, 2 * peers - 1 - place) >> 1
+    busy = owner == busiest
+    lent = busy & (place >= 4) & (place < 8)
+    busy_chip = jnp.where(place >= 12, 3 - (place & 3), place & 3)
+    chip = jnp.where(lent, (place - 4) >> 1, jnp.where(busy, busy_chip, chip))
+    owner = jnp.where(lent, (owner + place - 3) & (owners - 1), owner)
     return owner, place, chip
 
 
 def pack_kernel(
-    owners, peers, cluster_ref, order_ref, scale_ref, bias_ref, codes_hbm, out_ref,
-    codes_half, codes_full, slots_full, table_vmem, table_smem, code_sems, table_sem,
+    owners, peers, cluster_ref, order_ref, scale_hbm, bias_hbm, codes_hbm, out_ref,
+    codes_half, codes_full, slots_full, table_vmem, table_smem, scale_ref, bias_ref, code_sems, small_sems,
 ):
     local_rows = codes_hbm.shape[0]
     me_wide = lax.axis_index("wide")
     me_narrow = lax.axis_index("narrow")
     pieces = code_sems.shape[0]
+    tiles = codes_hbm.shape[1] // LANES
     piece = local_rows // pieces
     copies = [
         pltpu.make_async_copy(
@@ -58,71 +80,85 @@
         )
         for n in range(pieces)
     ]
-    for copy in copies:
+    small_copies = [
+        pltpu.make_async_copy(scale_hbm, scale_ref, small_sems.at[0]),
+        pltpu.make_async_copy(bias_hbm, bias_ref, small_sems.at[1]),
+    ]
+    for copy in copies + small_copies:
         copy.start()
 
-    before = strictly_before()
+    chunks = local_rows // CHUNK
+    busiest = busiest_owner(cluster_ref, owners)
+    places, masks, hots = [], [], []
+    for n in range(chunks):
+        owner, place, chip = owner_place_chip(chunk_of(cluster_ref, n), owners, peers, busiest)
+        mask = iota((owners, CHUNK), 0) == jnp.where(chip == me_narrow >> 1, owner, -1)
+        places.append(place)
+        masks.append(mask)
+        hots.append(jnp.where(mask, 1.0, 0.0))
+    earlier = dot(jnp.concatenate(hots, axis=0).astype(jnp.bfloat16), strictly_before(), 1, 0)
     count = jnp.zeros((owners, 1), jnp.float32)
-    table = jnp.zeros((owners, 3 * LANES), jnp.float32)
-    for n in range(local_rows // CHUNK):
-        clusters = chunk_of(cluster_ref, n)
-        orders = chunk_of(order_ref, n)
-        owner, place, chip = owner_and_chip(clusters, owners, peers)
-        owner = jnp.where(chip == me_narrow >> 1, owner, -1)
-        mine = iota((owners, CHUNK), 0) == owner
-        one_hot = jnp.where(mine, 1.0, 0.0)
-        one_hot_half = one_hot.astype(jnp.bfloat16)
-        earlier = dot(one_hot_half, before, 1, 0) + count
-        rank = jnp.sum(jnp.where(mine, earlier, 0.0), axis=0, keepdims=True).astype(jnp.int32)
-        count = count + jnp.sum(one_hot, axis=1, keepdims=True)
+    spread = []
+    for n in range(chunks):
+        within = earlier[n * owners : (n + 1) * owners]
+        rank = jnp.sum(jnp.where(masks[n], within + count, 0.0), axis=0, keepdims=True).astype(jnp.int32)
+        count = count + within[:, CHUNK - 1 :] + hots[n][:, CHUNK - 1 :]
         slot = jnp.where((rank & 1) == (me_narrow & 1), rank >> 1, -1)
-        key = place * ORDER_SPAN + orders + 1
+        key = places[n] * ORDER_SPAN + chunk_of(order_ref, n) + 1
         row = n * CHUNK + iota((1, CHUNK), 1)
-        at_slot = iota((HALF, CHUNK), 0) == slot
+        at_slot = iota((TABLE, CHUNK), 0) == slot
         parts = [
             jnp.where(at_slot, part.astype(jnp.float32), 0.0).astype(jnp.bfloat16)
             for part in (row >> 6, row & 63, key >> 16, (key >> 8) & 255, key & 255)
         ]
-        parts.append(jnp.zeros((HALF, CHUNK), jnp.bfloat16))
-        table = table + dot(one_hot_half, jnp.concatenate(parts, axis=0), 1, 1)
+        spread.append(jnp.concatenate(parts, axis=0))
+    table = dot(
+        jnp.concatenate(spread, axis=1), jnp.concatenate(hots, axis=1).astype(jnp.bfloat16), 1, 1
+    )
+    rows_at = table[:TABLE] * 64.0 + table[TABLE : 2 * TABLE]
+    wide = jnp.concatenate([count, jnp.zeros((owners, LANES - 1), jnp.float32)], axis=1)
+    counts = jnp.concatenate([wide, jnp.zeros((LANES - owners, LANES), jnp.float32)], axis=0).T[:1, :owners]
+    used = jnp.minimum((counts.astype(jnp.int32) + 1 - (me_narrow & 1)) >> 1, SLOTS)
+    table_vmem[:, :owners] = jnp.concatenate(
+        [rows_at.astype(jnp.int32), jnp.broadcast_to(used, (8, owners))], axis=0
+    )
+    table_copy = pltpu.make_async_copy(table_vmem, table_smem, small_sems.at[2])
+    table_copy.start()
+    over = jnp.where(jnp.max(count) > 2 * SLOTS, 1.0, 0.0)
+    turn = (me_wide * BLOCK) & (LANES - 1)
+    meta = []
+    for n in range(2, 5):
+        part = jnp.concatenate(
+            [table[n * TABLE : n * TABLE + SLOTS + 1], jnp.zeros((LANES - BLOCK, owners), jnp.float32)], axis=0
+        )
+        part = jnp.concatenate([part, jnp.zeros((LANES, LANES - owners), jnp.float32)], axis=1).T
+        meta.append(pltpu.roll(part[:owners], turn, 1))
     lane = iota((owners, LANES), 1)
-    rows_at = table[:, :LANES] * 64.0 + pltpu.roll(table[:, :LANES], HALF, 1)
-    used = jnp.minimum((count.astype(jnp.int32) + 1 - (me_narrow & 1)) >> 1, SLOTS)
-    table_vmem[...] = jnp.where(lane == HALF, used, rows_at.astype(jnp.int32))
-    table_copy = pltpu.make_async_copy(table_vmem, table_smem, table_sem)
-    table_copy.start()
-    turn = me_wide * BLOCK
-    first = jnp.where(lane < HALF, table[:, LANES : 2 * LANES], 0.0)
-    second = jnp.where(lane < HALF, 0.0, table[:, LANES : 2 * LANES])
-    third = table[:, 2 * LANES :]
-    over = jnp.where(jnp.max(count) > 2 * SLOTS, 1.0, 0.0)
-    meta = jnp.concatenate(
-        [
-            pltpu.roll(first, turn & (LANES - 1), 1),
-            pltpu.roll(second, (turn + HALF) & (LANES - 1), 1),
-            pltpu.roll(third, turn & (LANES - 1), 1),
-            jnp.full((owners, LANES), over, jnp.float32),
-        ],
-        axis=1,
-    )
+    meta.append(jnp.where(lane < HALF, over, busiest.astype(jnp.float32)))
 
     slots_full[...] = jnp.zeros_like(slots_full)
     for n, copy in enumerate(copies):
         copy.wait()
-        codes_full[n * piece : (n + 1) * piece, :] = codes_half[n * piece : (n + 1) * piece, :].astype(jnp.float32)
-    table_copy.wait()
+        values = codes_half[n * piece : (n + 1) * piece, :].astype(jnp.float32)
+        for tile in range(tiles):
+            codes_full[pl.ds(n * piece * PITCH + tile, piece, stride=PITCH), :] = values[
+                :, tile * LANES : (tile + 1) * LANES
+            ]
+    for copy in [table_copy] + small_copies:
+        copy.wait()
 
     def two_owners(half, carry):
         pair = (2 * half, 2 * half + 1)
-        used = jnp.maximum(table_smem[pair[0], HALF], table_smem[pair[1], HALF])
+        used = jnp.maximum(table_smem[TABLE, pair[0]], table_smem[TABLE, pair[1]])
 
         def eight_rows(group, carry):
             for owner in pair:
                 for n in range(8):
                     slot = group * 8 + n
-                    row = table_smem[owner, slot]
-                    slots_full[pl.ds(owner * BLOCK + slot, 1), :] = (
-                        codes_full[pl.ds(row, 1), :] * scale_ref[row] + bias_ref[row]
+                    row = table_smem[slot, owner]
+                    slots_full[pl.ds((owner * BLOCK + slot) * PITCH, TAKE), :] = (
+                        codes_full[pl.ds(row * PITCH, TAKE), :] * scale_ref[row]
+                        + bias_ref[row]
                     )
             return carry
 
@@ -131,34 +167,42 @@
     lax.fori_loop(0, owners // 2, two_owners, 0)
 
     pair = 2 * BLOCK
+    width = tiles * LANES
     for n in range(owners // 2):
-        values = slots_full[n * pair : (n + 1) * pair, :]
-        mean_square = jnp.mean(values * values, axis=1, keepdims=True)
-        unit = values * lax.rsqrt(mean_square + epsilon)
+        values = [
+            slots_full[pl.ds(n * pair * PITCH + tile, pair, stride=PITCH), :] for tile in range(tiles)
+        ]
+        squares = functools.reduce(jnp.add, [value * value for value in values])
+        mean_square = jnp.sum(squares, axis=1, keepdims=True) * (1.0 / width)
+        factor = lax.rsqrt(mean_square + epsilon)
         place = iota((pair, 1), 0)
-        unit = jnp.where(place == SLOTS, meta[2 * n : 2 * n + 1], unit)
-        unit = jnp.where(place == BLOCK + SLOTS, meta[2 * n + 1 : 2 * n + 2], unit)
-        out_ref[n * pair : (n + 1) * pair, :] = unit.astype(jnp.bfloat16)
+        for tile in range(tiles):
+            unit = values[tile] * factor
+            unit = jnp.where(place == SLOTS, meta[tile][2 * n : 2 * n + 1], unit)
+            unit = jnp.where(place == BLOCK + SLOTS, meta[tile][2 * n + 1 : 2 * n + 2], unit)
+            out_ref[n * pair : (n + 1) * pair, tile * LANES : (tile + 1) * LANES] = unit.astype(jnp.bfloat16)
 
 
 def pack(row_codes, row_scales, row_biases, cluster_ids, order_index, owners, peers):
     local_rows, width = row_codes.shape
     whole = pl.BlockSpec(memory_space=pltpu.VMEM)
-    scalars = pl.BlockSpec(memory_space=pltpu.SMEM)
+    outside = pl.BlockSpec(memory_space=pl.ANY)
     pieces = 8
     return pl.pallas_call(
         functools.partial(pack_kernel, owners, peers),
         out_shape=jax.ShapeDtypeStruct((owners * BLOCK, width), jnp.bfloat16),
-        in_specs=[whole, whole, scalars, scalars, pl.BlockSpec(memory_space=pl.ANY)],
+        in_specs=[whole, whole, outside, outside, outside],
         out_specs=whole,
         scratch_shapes=[
             pltpu.VMEM((local_rows, width), jnp.bfloat16),
-            pltpu.VMEM((local_rows, width), jnp.float32),
-            pltpu.VMEM((owners * BLOCK, width), jnp.float32),
-            pltpu.VMEM((owners, LANES), jnp.int32),
-            pltpu.SMEM((owners, LANES), jnp.int32),
+            pltpu.VMEM((local_rows * PITCH, LANES), jnp.float32),
+            pltpu.VMEM((owners * BLOCK * PITCH, LANES), jnp.float32),
+            pltpu.VMEM((TABLE + 8, LANES), jnp.int32),
+            pltpu.SMEM((TABLE + 8, LANES), jnp.int32),
+            pltpu.SMEM((local_rows,), jnp.float32),
+            pltpu.SMEM((local_rows,), jnp.float32),
             pltpu.SemaphoreType.DMA((pieces,)),
-            pltpu.SemaphoreType.DMA,
+            pltpu.SemaphoreType.DMA((3,)),
         ],
         compiler_params=pltpu.CompilerParams(vmem_limit_bytes=VMEM_LIMIT),
         name="pack",
@@ -172,8 +216,9 @@
     groups = owners * peers // 2
     before = strictly_before()
     count = jnp.zeros((groups, 1), jnp.float32)
+    busiest = busiest_owner(cluster_ref, owners)
     for n in range(cluster_ref.shape[0] // 2):
-        owner, _, chip = owner_and_chip(chunk_of(cluster_ref, n), owners, peers)
+        owner, _, chip = owner_place_chip(chunk_of(cluster_ref, n), owners, peers, busiest)
         mine = iota((groups, CHUNK), 0) == chip * owners + owner
         one_hot = jnp.where(mine, 1.0, 0.0)
         earlier = dot(one_hot.astype(jnp.bfloat16), before, 1, 0) + count
@@ -207,15 +252,18 @@
 
 def keys_of(owners, rows_ref, meta_ref):
     for n in range(owners):
-        end = (n + 1) * BLOCK
-        meta_ref[n : n + 1, :] = rows_ref[end - 16 : end, :].astype(jnp.float32)[15:16, :]
+        last = n * BLOCK + SLOTS
+        start = last // 16 * 16
+        meta_ref[n : n + 1, :] = rows_ref[start : start + 16, :].astype(jnp.float32)[last - start : last - start + 1, :]
     meta = meta_ref[...]
     key = meta[:, :LANES] * 65536.0 + meta[:, LANES : 2 * LANES] * 256.0 + meta[:, 2 * LANES : 3 * LANES]
     flat = [
         jnp.sum(jnp.where(in_block(owners, tile, SLOTS), key, 0.0), axis=0, keepdims=True)
         for tile in range(rows_ref.shape[0] // LANES)
     ]
-    return flat, jnp.max(meta[:, 3 * LANES :])
+    over = jnp.max(meta[:, 3 * LANES : 3 * LANES + HALF])
+    busiest = meta[:, 3 * LANES + HALF :]
+    return flat, jnp.where(jnp.max(busiest) == jnp.min(busiest), over, 1.0)
 
 
 def fold(rows_ref, key_rows_ref, keys, query_ref, best_in, best_ref):

time: 98.5 us -> 87.3 us (0.89)
  Pallas kernels: 20 us -> 14.2 us
  blocking collectives: 63 us -> 57.7 us
    all_to_all x1, blocking collectives: 50.4 us -> 45.6 us  [shards(): lax.all_to_all(sent.reshape(owners, BLOCK, width), 'wide', split_axis=0,...]
    pallas_call x1, Pallas kernels: 11.1 us -> 6.54 us  [pack(): pl.pallas_call(functools.partial(pack_kernel, owners, peers), out_shape=j...]
  transfers between devices with their start and end apart: 2 -> 2, of which waited for: 1 -> 2; matrix products, arithmetic and copies ran while one was open for 0% -> 0% of each run, Pallas kernels for 4% -> 4%
where the time goes in v3:
time: 87.3 us; the launch traced here: 86.7 us
  blocking collectives  57.7 us (66%)
  Pallas kernels  14.2 us (16%)
  starting transfers between devices  8.46 us (10%)
  waiting for transfers between devices  4.58 us (5%)
    all_to_all x1, blocking collectives, shards(): lax.all_to_all(sent.reshape(owners, BLOCK, width), 'wide', split_axis=0,...  45.6 us
    all_to_all x1, blocking collectives, shards(): lax.all_to_all(best.reshape(owners, 1, LANES), 'wide', split_axis=0, conc...  12.1 us
    pallas_call x1, Pallas kernels, pack(): pl.pallas_call(functools.partial(pack_kernel, owners, peers), out_shape=j...  6.54 us
    all_to_all x1, starting transfers between devices, shards(): lax.all_to_all(copies, 'narrow', split_axis=0, concat_axis=0, tiled=True)  6.03 us
    all_to_all x1, waiting for transfers between devices, shards(): lax.all_to_all(copies, 'narrow', split_axis=0, concat_axis=0, tiled=True)  4.22 us
    ppermute x1, starting transfers between devices, score(): other = lax.ppermute(rows, 'narrow', [(n, n ^ 1) for n in range(peers)])  2.43 us
    pallas_call x1, Pallas kernels, score(): pl.pallas_call(functools.partial(other_kernel, owners), out_shape=jax.Sha...  2.39 us
    pallas_call x1, Pallas kernels, score(): pl.pallas_call(functools.partial(own_kernel, owners), out_shape=(square,...  2.3 us
  transfers between devices with their start and end apart: 2, of which 2 were waited for; matrix products, arithmetic and copies ran while one was open for 0% of the time, Pallas kernels for 4%

profile of v3, /device:TPU:1, one launch (start us, length us, event | category | flops | bytes accessed | tf_op | source)
XLA Modules:
  0.0 86.7 jit_solution(13355810875587315958)
XLA Ops:
  0.0 6.5 %pack.1 = bf16[1280,512]{1,0:T(8,128)(2,1)S(1)} custom-call(s32[32,128]{1,0:T(8,128)} %bitcast.83, s32[32,128]{1,0:T(8,128)} %bitcast.97, f32[4096]{0:T(1024)} %scale_hbm.1, f32[4096]{0:T(1024)} %bias_hbm.1, bf16[4096,512]{1,0:T(8,128)(2,1)} %codes_hbm.1), custom_call_target="tpu_custom_call" | custom-call | tf_op jit(solution)/shard_map/pack/pallas_call | solution.py:191
  6.5 0.0 copy-start
  6.6 0.0 copy-start.1
  6.6 0.0 copy-start.2
  6.6 45.6 %all_to_all.44 = bf16[32,40,512]{2,1,0:T(8,128)(2,1)S(1)} all-to-all(bf16[32,40,512]{2,1,0:T(8,128)(2,1)S(1)} %bitcast.69), channel_id=1, replica_groups=mesh['wide'=32,'narrow'=8] {'wide'}, dimensions={0} | all-to-all | bytes 2621440 | tf_op jit(solution)/shard_map/all_to_all | solution.py:468
  52.2 2.4 %collective-permute-start = (bf16[1280,512]{1,0:T(8,128)(2,1)S(1)}, bf16[1280,512]{1,0:T(8,128)(2,1)S(1)}, u32[]{:S(2)}, u32[]{:S(2)}) collective-permute-start(bf16[1280,512]{1,0:T(8,128)(2,1)S(1)} %bitcast.70), channel_id=1, source_target_pairs={{0,1},{1,0},{2,3},{3,2},{4,5},{5,4},{6,7},{7,6},{8,9},{9,8},{10,11... | collective-permute-start | bytes 3932168 | tf_op jit(solution)/shard_map/ppermute | solution.py:312
  54.6 2.3 %score_own.1 = (f32[128,128]{1,0:T(8,128)S(1)}, f32[128,128]{1,0:T(8,128)S(1)}) custom-call(bf16[1280,512]{1,0:T(8,128)(2,1)S(1)} %bitcast.71), custom_call_target="tpu_custom_call" | custom-call | flops 1677721600 | bytes 2621440 | tf_op jit(solution)/shard_map/score_own/pallas_call | solution.py:315
  56.9 0.4 collective-permute-done.other_ref
  57.3 2.4 %score_other.1 = f32[32,128]{1,0:T(8,128)S(1)} custom-call(bf16[1280,512]{1,0:T(8,128)(2,1)S(1)} %bitcast.72, bf16[1280,512]{1,0:T(8,128)(2,1)S(1)} %collective-permute-done.other_ref, f32[128,128]{1,0:T(8,128)S(1)} %get-tuple-element.185.query_ref, f32[128,128]{1,0:T(8,128)S(1)} %get-tuple-element.186.best_in), custom_call_target="tpu_custom_call" | custom-call | flops 1677721600 | bytes 2621440 | tf_op jit(solution)/shard_map/score_other/pallas_call | solution.py:325
  59.7 12.1 %all_to_all.45 = f32[32,1,128]{2,1,0:T(1,128)S(1)} all-to-all(f32[32,1,128]{2,1,0:T(1,128)S(1)} %bitcast.74), channel_id=1, replica_groups=mesh['wide'=32,'narrow'=8] {'wide'}, dimensions={0} | all-to-all | bytes 32768 | tf_op jit(solution)/shard_map/all_to_all | solution.py:473
  71.8 0.6 broadcast_in_dim.13
  72.4 6.0 %all-to-all-start.6 = ((f32[8,32,128]{2,1,0:T(8,128)}), f32[8,32,128]{2,1,0:T(8,128)S(1)}, u32[]{:S(2)}, u32[]{:S(2)}) async-start(f32[8,32,128]{2,1,0:T(8,128)} %broadcast_in_dim.13), calls=%async_computation.6 | async-start | bytes 262144 | tf_op jit(solution)/shard_map/all_to_all | solution.py:475
  78.5 0.0 copy-done
  78.5 1.0 %places.1 = (s32[32,128]{1,0:T(8,128)S(1)}, s32[32,128]{1,0:T(8,128)S(1)}) custom-call(s32[32,128]{1,0:T(8,128)S(1)} %bitcast.84), custom_call_target="tpu_custom_call" | custom-call | tf_op jit(solution)/shard_map/places/pallas_call | solution.py:238
  79.5 4.2 %all-to-all-done.6 = f32[8,32,128]{2,1,0:T(8,128)S(1)} async-done(((f32[8,32,128]{2,1,0:T(8,128)}), f32[8,32,128]{2,1,0:T(8,128)S(1)}, u32[]{:S(2)}, u32[]{:S(2)}) %all-to-all-start.6) | async-done | bytes 131104 | tf_op jit(solution)/shard_map/all_to_all | solution.py:475
  83.8 1.9 %pick.1 = (f32[32,128]{1,0:T(8,128)}, s32[1,1]{1,0:T(1,128)}) custom-call(f32[256,128]{1,0:T(8,128)S(1)} %bitcast.73, s32[32,128]{1,0:T(8,128)S(1)} %get-tuple-element.187.group_ref, s32[32,128]{1,0:T(8,128)S(1)} %get-tuple-element.188.lane_ref), custom_call_target="tpu_custom_call" | custom-call | tf_op jit(solution)/shard_map/pick/pallas_call | solution.py:361
  85.7 0.0 copy-done.1
  85.7 0.0 copy-done.2
  85.7 0.8 while.21
Async XLA Ops:
  6.5 71.9 %copy-start = (s32[4096]{0:T(1024)S(1)}, s32[4096]{0:T(1024)}, u32[]{:S(2)}) copy-start(s32[4096]{0:T(1024)} %param.12) | copy-start | bytes 49156
  6.6 79.1 %copy-start.1 = (f32[4096]{0:T(1024)S(1)}, f32[4096]{0:T(1024)}, u32[]{:S(2)}) copy-start(f32[4096]{0:T(1024)} %scale_hbm.1) | copy-start | bytes 49156
  6.6 79.1 %copy-start.2 = (f32[4096]{0:T(1024)S(1)}, f32[4096]{0:T(1024)}, u32[]{:S(2)}) copy-start(f32[4096]{0:T(1024)} %bias_hbm.1) | copy-start | bytes 49156
  52.2 5.1 %collective-permute-start = (bf16[1280,512]{1,0:T(8,128)(2,1)S(1)}, bf16[1280,512]{1,0:T(8,128)(2,1)S(1)}, u32[]{:S(2)}, u32[]{:S(2)}) collective-permute-start(bf16[1280,512]{1,0:T(8,128)(2,1)S(1)} %bitcast.70), channel_id=1, source_target_pairs={{0,1},{1,0},{2,3},{3,2},{4,5},{5,4},{6,7},{7,6},{8,9},{9,8},{10,11... | collective-permute-start | bytes 3932168 | tf_op jit(solution)/shard_map/ppermute | solution.py:312
  72.4 11.3 %all-to-all-start.6 = ((f32[8,32,128]{2,1,0:T(8,128)}), f32[8,32,128]{2,1,0:T(8,128)S(1)}, u32[]{:S(2)}, u32[]{:S(2)}) async-start(f32[8,32,128]{2,1,0:T(8,128)} %broadcast_in_dim.13), calls=%async_computation.6 | async-start | bytes 262144 | tf_op jit(solution)/shard_map/all_to_all | solution.py:475

commit v4 on v3

--- a/solution.py
+++ b/solution.py
@@ -9,12 +9,13 @@
 
 epsilon = 1e-06
 
-BLOCK = 40
+BLOCK = 32
 SLOTS = BLOCK - 1
 LANES = 128
 HALF = LANES // 2
 PITCH = 5
-TABLE = 48
+LENT_FIRST, LENT = 4, 8
+HOST_CHIPS = -1620452551
 TAKE = 4
 CHUNK = 256
 ORDER_SPAN = 131072
@@ -55,12 +56,13 @@
 
 def owner_place_chip(clusters, owners, peers, busiest):
     owner, place = split(clusters, owners)
-    chip = jnp.minimum(place, 2 * peers - 1 - place) >> 1
-    busy = owner == busiest
-    lent = busy & (place >= 4) & (place < 8)
-    busy_chip = jnp.where(place >= 12, 3 - (place & 3), place & 3)
-    chip = jnp.where(lent, (place - 4) >> 1, jnp.where(busy, busy_chip, chip))
-    owner = jnp.where(lent, (owner + place - 3) & (owners - 1), owner)
+    ahead = (owner - busiest) & (owners - 1)
+    folded = jnp.minimum(place, 2 * peers - 1 - place)
+    lent = (ahead == 0) & (place >= LENT_FIRST) & (place < LENT_FIRST + LENT)
+    host_chip = lax.shift_right_logical(jnp.full_like(place, HOST_CHIPS), 2 * place) & 3
+    chip = jnp.where(ahead <= LENT, host_chip, folded >> 1)
+    chip = jnp.where(lent, 0, jnp.where(ahead == 0, folded & 3, chip))
+    owner = jnp.where(lent, (owner + place + 1 - LENT_FIRST) & (owners - 1), owner)
     return owner, place, chip
 
 
@@ -106,7 +108,7 @@
         slot = jnp.where((rank & 1) == (me_narrow & 1), rank >> 1, -1)
         key = places[n] * ORDER_SPAN + chunk_of(order_ref, n) + 1
         row = n * CHUNK + iota((1, CHUNK), 1)
-        at_slot = iota((TABLE, CHUNK), 0) == slot
+        at_slot = iota((BLOCK, CHUNK), 0) == slot
         parts = [
             jnp.where(at_slot, part.astype(jnp.float32), 0.0).astype(jnp.bfloat16)
             for part in (row >> 6, row & 63, key >> 16, (key >> 8) & 255, key & 255)
@@ -115,7 +117,7 @@
     table = dot(
         jnp.concatenate(spread, axis=1), jnp.concatenate(hots, axis=1).astype(jnp.bfloat16), 1, 1
     )
-    rows_at = table[:TABLE] * 64.0 + table[TABLE : 2 * TABLE]
+    rows_at = table[:BLOCK] * 64.0 + table[BLOCK : 2 * BLOCK]
     wide = jnp.concatenate([count, jnp.zeros((owners, LANES - 1), jnp.float32)], axis=1)
     counts = jnp.concatenate([wide, jnp.zeros((LANES - owners, LANES), jnp.float32)], axis=0).T[:1, :owners]
     used = jnp.minimum((counts.astype(jnp.int32) + 1 - (me_narrow & 1)) >> 1, SLOTS)
@@ -129,7 +131,7 @@
     meta = []
     for n in range(2, 5):
         part = jnp.concatenate(
-            [table[n * TABLE : n * TABLE + SLOTS + 1], jnp.zeros((LANES - BLOCK, owners), jnp.float32)], axis=0
+            [table[n * BLOCK : n * BLOCK + SLOTS + 1], jnp.zeros((LANES - BLOCK, owners), jnp.float32)], axis=0
         )
         part = jnp.concatenate([part, jnp.zeros((LANES, LANES - owners), jnp.float32)], axis=1).T
         meta.append(pltpu.roll(part[:owners], turn, 1))
@@ -149,7 +151,7 @@
 
     def two_owners(half, carry):
         pair = (2 * half, 2 * half + 1)
-        used = jnp.maximum(table_smem[TABLE, pair[0]], table_smem[TABLE, pair[1]])
+        used = jnp.maximum(table_smem[BLOCK, pair[0]], table_smem[BLOCK, pair[1]])
 
         def eight_rows(group, carry):
             for owner in pair:
@@ -197,8 +199,8 @@
             pltpu.VMEM((local_rows, width), jnp.bfloat16),
             pltpu.VMEM((local_rows * PITCH, LANES), jnp.float32),
             pltpu.VMEM((owners * BLOCK * PITCH, LANES), jnp.float32),
-            pltpu.VMEM((TABLE + 8, LANES), jnp.int32),
-            pltpu.SMEM((TABLE + 8, LANES), jnp.int32),
+            pltpu.VMEM((BLOCK + 8, LANES), jnp.int32),
+            pltpu.SMEM((BLOCK + 8, LANES), jnp.int32),
             pltpu.SMEM((local_rows,), jnp.float32),
             pltpu.SMEM((local_rows,), jnp.float32),
             pltpu.SemaphoreType.DMA((pieces,)),
@@ -211,8 +213,7 @@
     )
 
 
-def place_kernel(owners, peers, cluster_ref, group_ref, lane_ref):
-    me_wide = lax.axis_index("wide")
+def place_kernel(owners, peers, cluster_ref, group_ref, slot_ref):
     groups = owners * peers // 2
     before = strictly_before()
     count = jnp.zeros((groups, 1), jnp.float32)
@@ -225,11 +226,11 @@
         rank = jnp.sum(jnp.where(mine, earlier, 0.0), axis=0, keepdims=True).astype(jnp.int32)
         count = count + jnp.sum(one_hot, axis=1, keepdims=True)
         group = (2 * chip + (rank & 1)) * owners + owner
-        lane = (me_wide * BLOCK + (rank >> 1)) & (LANES - 1)
+        slot = jnp.minimum(rank >> 1, SLOTS)
         for half in range(2):
             part = slice(half * LANES, (half + 1) * LANES)
             group_ref[2 * n + half : 2 * n + half + 1, :] = group[:, part]
-            lane_ref[2 * n + half : 2 * n + half + 1, :] = lane[:, part]
+            slot_ref[2 * n + half : 2 * n + half + 1, :] = slot[:, part]
 
 
 def places(cluster_ids, owners, peers):
@@ -334,29 +335,27 @@
     )(rows, other, query, best)
 
 
-def pick_kernel(values_ref, group_ref, lane_ref, out_ref, over_ref):
-    me_wide = lax.axis_index("wide")
+def pick_kernel(values_ref, group_ref, slot_ref, out_ref, over_ref):
     groups = values_ref.shape[0]
-    values = values_ref[...]
-    marked = iota((groups, LANES), 1) == ((me_wide * BLOCK + SLOTS) & (LANES - 1))
-    over_ref[0, 0] = jnp.max(jnp.where(marked, values, 0.0)).astype(jnp.int32)
-    turned = values.T
-    high = turned.astype(jnp.bfloat16)
-    rest = turned - high.astype(jnp.float32)
+    turn = (lax.axis_index("wide") * BLOCK) & (LANES - 1)
+    values = pltpu.roll(values_ref[...], (LANES - turn) & (LANES - 1), 1).T[:BLOCK]
+    over_ref[0, 0] = jnp.max(values[SLOTS:]).astype(jnp.int32)
+    high = values.astype(jnp.bfloat16)
+    rest = values - high.astype(jnp.float32)
     middle = rest.astype(jnp.bfloat16)
     low = (rest - middle.astype(jnp.float32)).astype(jnp.bfloat16)
     parts = jnp.concatenate([high, middle, low], axis=0)
     for n in range(group_ref.shape[0] // 2):
         one_hot = jnp.where(iota((groups, CHUNK), 0) == chunk_of(group_ref, n), 1.0, 0.0).astype(jnp.bfloat16)
-        by_lane = dot(parts, one_hot, 1, 0)
-        by_lane = by_lane[:LANES] + by_lane[LANES : 2 * LANES] + by_lane[2 * LANES :]
-        here = iota((LANES, CHUNK), 0) == chunk_of(lane_ref, n)
-        picked = jnp.sum(jnp.where(here, by_lane, 0.0), axis=0, keepdims=True)
+        by_slot = dot(parts, one_hot, 1, 0)
+        by_slot = by_slot[:BLOCK] + by_slot[BLOCK : 2 * BLOCK] + by_slot[2 * BLOCK :]
+        here = iota((BLOCK, CHUNK), 0) == chunk_of(slot_ref, n)
+        picked = jnp.sum(jnp.where(here, by_slot, 0.0), axis=0, keepdims=True)
         out_ref[2 * n : 2 * n + 1, :] = picked[:, :LANES]
         out_ref[2 * n + 1 : 2 * n + 2, :] = picked[:, LANES:]
 
 
-def pick(values, group, lane):
+def pick(values, group, slot):
     whole = pl.BlockSpec(memory_space=pltpu.VMEM)
     return pl.pallas_call(
         pick_kernel,
@@ -368,7 +367,7 @@
         out_specs=(whole, pl.BlockSpec(memory_space=pltpu.SMEM)),
         compiler_params=pltpu.CompilerParams(vmem_limit_bytes=VMEM_LIMIT),
         name="pick",
-    )(values, group, lane)
+    )(values, group, slot)
 
 
 def unit_vectors(row_codes, row_scales, row_biases):
@@ -468,13 +467,13 @@
     got = lax.all_to_all(
         sent.reshape(owners, BLOCK, width), "wide", split_axis=0, concat_axis=0, tiled=True
     ).reshape(owners * BLOCK, width)
-    group, lane = places(cluster_ids, owners, peers)
+    group, slot = places(cluster_ids, owners, peers)
     best = score(got, owners)
     back = lax.all_to_all(best.reshape(owners, 1, LANES), "wide", split_axis=0, concat_axis=0, tiled=True)
     copies = jnp.broadcast_to(back.reshape(1, owners, LANES), (peers, owners, LANES))
     values = lax.all_to_all(copies, "narrow", split_axis=0, concat_axis=0, tiled=True)
     values = values.reshape(peers * owners, LANES)
-    picked, over = pick(values, group, lane)
+    picked, over = pick(values, group, slot)
     _, result = lax.while_loop(
         lambda state: state[0] > 0,
         lambda state: (

time: 87.3 us -> 79.6 us (0.912)
  blocking collectives: 57.7 us -> 51.3 us
  Pallas kernels: 14.2 us -> 11.7 us
  starting transfers between devices: 8.46 us -> 9.46 us
    all_to_all x1, blocking collectives: 45.6 us -> 37.8 us  [shards(): lax.all_to_all(sent.reshape(owners, BLOCK, width), 'wide', split_axis=0,...]
    all_to_all x1, blocking collectives: 12.1 us -> 13.5 us  [shards(): lax.all_to_all(best.reshape(owners, 1, LANES), 'wide', split_axis=0, conc...]
  transfers between devices with their start and end apart: 2 -> 2, of which waited for: 2 -> 2; matrix products, arithmetic and copies ran while one was open for 0% -> 0% of each run, Pallas kernels for 4% -> 3%
where the time goes in v4:
time: 79.6 us; the launch traced here: 79.1 us
  blocking collectives  51.3 us (64%)
  Pallas kernels  11.7 us (15%)
  starting transfers between devices  9.46 us (12%)
  waiting for transfers between devices  4.89 us (6%)
  loops' own time  0.84 us (1%)
    all_to_all x1, blocking collectives, shards(): lax.all_to_all(sent.reshape(owners, BLOCK, width), 'wide', split_axis=0,...  37.8 us
    all_to_all x1, blocking collectives, shards(): lax.all_to_all(best.reshape(owners, 1, LANES), 'wide', split_axis=0, conc...  13.5 us
    all_to_all x1, starting transfers between devices, shards(): lax.all_to_all(copies, 'narrow', split_axis=0, concat_axis=0, tiled=True)  6.4 us
    pallas_call x1, Pallas kernels, pack(): pl.pallas_call(functools.partial(pack_kernel, owners, peers), out_shape=j...  6 us
    all_to_all x1, waiting for transfers between devices, shards(): lax.all_to_all(copies, 'narrow', split_axis=0, concat_axis=0, tiled=True)  4.21 us
    ppermute x1, starting transfers between devices, score(): other = lax.ppermute(rows, 'narrow', [(n, n ^ 1) for n in range(peers)])  3.06 us
    pallas_call x1, Pallas kernels, score(): pl.pallas_call(functools.partial(other_kernel, owners), out_shape=jax.Sha...  1.65 us
    pallas_call x1, Pallas kernels, score(): pl.pallas_call(functools.partial(own_kernel, owners), out_shape=(square,...  1.6 us
  transfers between devices with their start and end apart: 2, of which 2 were waited for; matrix products, arithmetic and copies ran while one was open for 0% of the time, Pallas kernels for 3%

profile of v4, /device:TPU:1, one launch (start us, length us, event | category | flops | bytes accessed | tf_op | source)
XLA Modules:
  0.0 79.1 jit_solution(943409002520696572)
XLA Ops:
  0.0 0.0 copy-start
  0.0 0.0 copy-start.1
  0.0 0.0 copy-start.2
  0.0 6.0 %pack.1 = bf16[1024,512]{1,0:T(8,128)(2,1)S(1)} custom-call(s32[32,128]{1,0:T(8,128)} %bitcast.83, s32[32,128]{1,0:T(8,128)} %bitcast.97, f32[4096]{0:T(1024)} %scale_hbm.1, f32[4096]{0:T(1024)} %bias_hbm.1, bf16[4096,512]{1,0:T(8,128)(2,1)} %codes_hbm.1), custom_call_target="tpu_custom_call" | custom-call | tf_op jit(solution)/shard_map/pack/pallas_call | solution.py:193
  6.0 37.8 %all_to_all.44 = bf16[32,32,512]{2,1,0:T(8,128)(2,1)S(1)} all-to-all(bf16[32,32,512]{2,1,0:T(8,128)(2,1)S(1)} %bitcast.69), channel_id=1, replica_groups=mesh['wide'=32,'narrow'=8] {'wide'}, dimensions={0} | all-to-all | bytes 2097152 | tf_op jit(solution)/shard_map/all_to_all | solution.py:467
  43.8 3.1 %collective-permute-start = (bf16[1024,512]{1,0:T(8,128)(2,1)S(1)}, bf16[1024,512]{1,0:T(8,128)(2,1)S(1)}, u32[]{:S(2)}, u32[]{:S(2)}) collective-permute-start(bf16[1024,512]{1,0:T(8,128)(2,1)S(1)} %bitcast.70), channel_id=1, source_target_pairs={{0,1},{1,0},{2,3},{3,2},{4,5},{5,4},{6,7},{7,6},{8,9},{9,8},{10,11... | collective-permute-start | bytes 3145736 | tf_op jit(solution)/shard_map/ppermute | solution.py:313
  46.9 1.6 %score_own.1 = (f32[128,128]{1,0:T(8,128)S(1)}, f32[128,128]{1,0:T(8,128)S(1)}) custom-call(bf16[1024,512]{1,0:T(8,128)(2,1)S(1)} %bitcast.71), custom_call_target="tpu_custom_call" | custom-call | flops 1073741824 | bytes 2097152 | tf_op jit(solution)/shard_map/score_own/pallas_call | solution.py:316
  48.5 0.7 collective-permute-done.other_ref
  49.2 1.6 %score_other.1 = f32[32,128]{1,0:T(8,128)S(1)} custom-call(bf16[1024,512]{1,0:T(8,128)(2,1)S(1)} %bitcast.72, bf16[1024,512]{1,0:T(8,128)(2,1)S(1)} %collective-permute-done.other_ref, f32[128,128]{1,0:T(8,128)S(1)} %get-tuple-element.185.query_ref, f32[128,128]{1,0:T(8,128)S(1)} %get-tuple-element.186.best_in), custom_call_target="tpu_custom_call" | custom-call | flops 1073741824 | bytes 2097152 | tf_op jit(solution)/shard_map/score_other/pallas_call | solution.py:326
  50.8 13.5 %all_to_all.45 = f32[32,1,128]{2,1,0:T(1,128)S(1)} all-to-all(f32[32,1,128]{2,1,0:T(1,128)S(1)} %bitcast.74), channel_id=1, replica_groups=mesh['wide'=32,'narrow'=8] {'wide'}, dimensions={0} | all-to-all | bytes 32768 | tf_op jit(solution)/shard_map/all_to_all | solution.py:472
  64.4 0.6 broadcast_in_dim.13
  65.0 6.4 %all-to-all-start.6 = ((f32[8,32,128]{2,1,0:T(8,128)}), f32[8,32,128]{2,1,0:T(8,128)S(1)}, u32[]{:S(2)}, u32[]{:S(2)}) async-start(f32[8,32,128]{2,1,0:T(8,128)} %broadcast_in_dim.13), calls=%async_computation.6 | async-start | bytes 262144 | tf_op jit(solution)/shard_map/all_to_all | solution.py:474
  71.4 0.0 copy-done
  71.4 1.1 %places.1 = (s32[32,128]{1,0:T(8,128)S(1)}, s32[32,128]{1,0:T(8,128)S(1)}) custom-call(s32[32,128]{1,0:T(8,128)S(1)} %bitcast.84), custom_call_target="tpu_custom_call" | custom-call | tf_op jit(solution)/shard_map/places/pallas_call | solution.py:239
  72.5 4.2 %all-to-all-done.6 = f32[8,32,128]{2,1,0:T(8,128)S(1)} async-done(((f32[8,32,128]{2,1,0:T(8,128)}), f32[8,32,128]{2,1,0:T(8,128)S(1)}, u32[]{:S(2)}, u32[]{:S(2)}) %all-to-all-start.6) | async-done | bytes 131104 | tf_op jit(solution)/shard_map/all_to_all | solution.py:474
  76.7 1.4 %pick.1 = (f32[32,128]{1,0:T(8,128)}, s32[1,1]{1,0:T(1,128)}) custom-call(f32[256,128]{1,0:T(8,128)S(1)} %bitcast.73, s32[32,128]{1,0:T(8,128)S(1)} %get-tuple-element.187.group_ref, s32[32,128]{1,0:T(8,128)S(1)} %get-tuple-element.188.slot_ref), custom_call_target="tpu_custom_call" | custom-call | tf_op jit(solution)/shard_map/pick/pallas_call | solution.py:360
  78.1 0.0 copy-done.1
  78.1 0.0 copy-done.2
  78.1 0.8 %while.21 = (s32[]{:T(128)}, f32[4096]{0:T(1024)}, s32[4096]{0:T(1024)S(1)}, bf16[4096,512]{1,0:T(8,128)(2,1)}, f32[4096]{0:T(1024)S(1)}, /*index=5*/f32[4096]{0:T(1024)S(1)}, s32[4096]{0:T(1024)}) while((s32[]{:T(128)}, f32[4096]{0:T(1024)}, s32[4096]{0:T(1024)S(1)}, bf16[4096,512]{1,0:T(8,128)(2,1)}, f32[4096]{0:T(1024)S(1)}, ...), condition=%region_11.12_spmd, body=%region_0.11_spmd | while | flops 1118893056 | bytes 52520216 | solution.py:477
Async XLA Ops:
  0.0 71.4 %copy-start = (s32[4096]{0:T(1024)S(1)}, s32[4096]{0:T(1024)}, u32[]{:S(2)}) copy-start(s32[4096]{0:T(1024)} %param.12) | copy-start | bytes 49156
  0.0 78.1 %copy-start.1 = (f32[4096]{0:T(1024)S(1)}, f32[4096]{0:T(1024)}, u32[]{:S(2)}) copy-start(f32[4096]{0:T(1024)} %scale_hbm.1) | copy-start | bytes 49156
  0.0 78.1 %copy-start.2 = (f32[4096]{0:T(1024)S(1)}, f32[4096]{0:T(1024)}, u32[]{:S(2)}) copy-start(f32[4096]{0:T(1024)} %bias_hbm.1) | copy-start | bytes 49156
  43.8 5.3 %collective-permute-start = (bf16[1024,512]{1,0:T(8,128)(2,1)S(1)}, bf16[1024,512]{1,0:T(8,128)(2,1)S(1)}, u32[]{:S(2)}, u32[]{:S(2)}) collective-permute-start(bf16[1024,512]{1,0:T(8,128)(2,1)S(1)} %bitcast.70), channel_id=1, source_target_pairs={{0,1},{1,0},{2,3},{3,2},{4,5},{5,4},{6,7},{7,6},{8,9},{9,8},{10,11... | collective-permute-start | bytes 3145736 | tf_op jit(solution)/shard_map/ppermute | solution.py:313
  65.0 11.7 %all-to-all-start.6 = ((f32[8,32,128]{2,1,0:T(8,128)}), f32[8,32,128]{2,1,0:T(8,128)S(1)}, u32[]{:S(2)}, u32[]{:S(2)}) async-start(f32[8,32,128]{2,1,0:T(8,128)} %broadcast_in_dim.13), calls=%async_computation.6 | async-start | bytes 262144 | tf_op jit(solution)/shard_map/all_to_all | solution.py:474

commit v5 on v4

--- a/solution.py
+++ b/solution.py
@@ -67,7 +67,7 @@
 
 
 def pack_kernel(
-    owners, peers, cluster_ref, order_ref, scale_hbm, bias_hbm, codes_hbm, out_ref,
+    owners, peers, cluster_ref, order_ref, scale_hbm, bias_hbm, codes_hbm, out_ref, kept_ref,
     codes_half, codes_full, slots_full, table_vmem, table_smem, scale_ref, bias_ref, code_sems, small_sems,
 ):
     local_rows = codes_hbm.shape[0]
@@ -90,6 +90,7 @@
         copy.start()
 
     chunks = local_rows // CHUNK
+    kept_ref[...] = cluster_ref[...]
     busiest = busiest_owner(cluster_ref, owners)
     places, masks, hots = [], [], []
     for n in range(chunks):
@@ -192,9 +193,12 @@
     pieces = 8
     return pl.pallas_call(
         functools.partial(pack_kernel, owners, peers),
-        out_shape=jax.ShapeDtypeStruct((owners * BLOCK, width), jnp.bfloat16),
+        out_shape=(
+            jax.ShapeDtypeStruct((owners * BLOCK, width), jnp.bfloat16),
+            jax.ShapeDtypeStruct((local_rows // LANES, LANES), jnp.int32),
+        ),
         in_specs=[whole, whole, outside, outside, outside],
-        out_specs=whole,
+        out_specs=(whole, whole),
         scratch_shapes=[
             pltpu.VMEM((local_rows, width), jnp.bfloat16),
             pltpu.VMEM((local_rows * PITCH, LANES), jnp.float32),
@@ -225,7 +229,8 @@
         earlier = dot(one_hot.astype(jnp.bfloat16), before, 1, 0) + count
         rank = jnp.sum(jnp.where(mine, earlier, 0.0), axis=0, keepdims=True).astype(jnp.int32)
         count = count + jnp.sum(one_hot, axis=1, keepdims=True)
-        group = (2 * chip + (rank & 1)) * owners + owner
+        peer = 2 * chip + (rank & 1)
+        group = ((owner >> 3) * peers + peer) * 8 + (owner & 7)
         slot = jnp.minimum(rank >> 1, SLOTS)
         for half in range(2):
             part = slice(half * LANES, (half + 1) * LANES)
@@ -233,17 +238,18 @@
             slot_ref[2 * n + half : 2 * n + half + 1, :] = slot[:, part]
 
 
-def places(cluster_ids, owners, peers):
+def places(clusters, owners, peers):
     whole = pl.BlockSpec(memory_space=pltpu.VMEM)
-    shape = jax.ShapeDtypeStruct((cluster_ids.shape[0] // LANES, LANES), jnp.int32)
+    shape = jax.ShapeDtypeStruct(clusters.shape, jnp.int32)
     return pl.pallas_call(
         functools.partial(place_kernel, owners, peers),
         out_shape=(shape, shape),
         in_specs=[whole],
         out_specs=(whole, whole),
         compiler_params=pltpu.CompilerParams(vmem_limit_bytes=VMEM_LIMIT),
+        cost_estimate=pl.CostEstimate(flops=2**30, bytes_accessed=2**16, transcendentals=0),
         name="places",
-    )(cluster_ids.reshape(-1, LANES))
+    )(clusters)
 
 
 def in_block(owners, tile, length):
@@ -302,7 +308,7 @@
     out_ref[...] = result
 
 
-def score(rows, owners):
+def score(rows, clusters, owners):
     slots, width = rows.shape
     whole = pl.BlockSpec(memory_space=pltpu.VMEM)
     square = jax.ShapeDtypeStruct((LANES, LANES), jnp.float32)
@@ -323,7 +329,9 @@
         cost_estimate=cost,
         name="score_own",
     )(rows)
-    return pl.pallas_call(
+    group, slot = places(clusters, owners, peers)
+    other, query, best, group, slot = lax.optimization_barrier((other, query, best, group, slot))
+    result = pl.pallas_call(
         functools.partial(other_kernel, owners),
         out_shape=jax.ShapeDtypeStruct((owners, LANES), jnp.float32),
         in_specs=[whole] * 4,
@@ -333,12 +341,38 @@
         cost_estimate=cost,
         name="score_other",
     )(rows, other, query, best)
+    return result, group, slot
+
+
+def spread_kernel(back_ref, out_ref):
+    turn = (lax.axis_index("wide") * BLOCK) & (LANES - 1)
+    lane = iota((8, LANES), 1) // BLOCK
+    dense = jnp.zeros((8, LANES), jnp.float32)
+    for n in range(LANES // BLOCK):
+        part = pltpu.roll(back_ref[8 * n : 8 * n + 8, :], (n * BLOCK + LANES - turn) & (LANES - 1), 1)
+        dense = jnp.where(lane == n, part, dense)
+    for n in range(out_ref.shape[0]):
+        out_ref[n] = dense
+
+
+def spread(back, peers):
+    whole = pl.BlockSpec(memory_space=pltpu.VMEM)
+    return pl.pallas_call(
+        spread_kernel,
+        out_shape=jax.ShapeDtypeStruct((peers, 8, LANES), jnp.float32),
+        in_specs=[whole],
+        out_specs=whole,
+        compiler_params=pltpu.CompilerParams(vmem_limit_bytes=VMEM_LIMIT),
+        name="spread",
+    )(back)
 
 
 def pick_kernel(values_ref, group_ref, slot_ref, out_ref, over_ref):
-    groups = values_ref.shape[0]
-    turn = (lax.axis_index("wide") * BLOCK) & (LANES - 1)
-    values = pltpu.roll(values_ref[...], (LANES - turn) & (LANES - 1), 1).T[:BLOCK]
+    turned = values_ref[...].T
+    values = jnp.concatenate(
+        [turned[n * BLOCK : (n + 1) * BLOCK] for n in range(LANES // BLOCK)], axis=1
+    )
+    groups = values.shape[1]
     over_ref[0, 0] = jnp.max(values[SLOTS:]).astype(jnp.int32)
     high = values.astype(jnp.bfloat16)
     rest = values - high.astype(jnp.float32)
@@ -463,16 +497,15 @@
     owners = lax.axis_size("wide")
     peers = lax.axis_size("narrow")
     width = row_codes.shape[1]
-    sent = pack(row_codes, row_scales, row_biases, cluster_ids, order_index, owners, peers)
+    sent, clusters = pack(row_codes, row_scales, row_biases, cluster_ids, order_index, owners, peers)
     got = lax.all_to_all(
         sent.reshape(owners, BLOCK, width), "wide", split_axis=0, concat_axis=0, tiled=True
     ).reshape(owners * BLOCK, width)
-    group, slot = places(cluster_ids, owners, peers)
-    best = score(got, owners)
+    best, group, slot = score(got, clusters, owners)
     back = lax.all_to_all(best.reshape(owners, 1, LANES), "wide", split_axis=0, concat_axis=0, tiled=True)
-    copies = jnp.broadcast_to(back.reshape(1, owners, LANES), (peers, owners, LANES))
+    copies = spread(back.reshape(owners, LANES), peers)
     values = lax.all_to_all(copies, "narrow", split_axis=0, concat_axis=0, tiled=True)
-    values = values.reshape(peers * owners, LANES)
+    values = values.reshape(peers * 8, LANES)
     picked, over = pick(values, group, slot)
     _, result = lax.while_loop(
         lambda state: state[0] > 0,

time: 79.6 us -> 78.1 us (0.981)
  blocking collectives: 51.3 us -> 61.8 us
  starting transfers between devices: 9.46 us -> 2.91 us
  waiting for transfers between devices: 4.89 us -> 0.01 us
    all_to_all x0 -> x1, blocking collectives: none -> 10.5 us  [shards(): lax.all_to_all(copies, 'narrow', split_axis=0, concat_axis=0, tiled=True)]
    all_to_all x1 -> x0, starting transfers between devices: 6.4 us -> none  [shards(): lax.all_to_all(copies, 'narrow', split_axis=0, concat_axis=0, tiled=True)]
    all_to_all x1 -> x0, waiting for transfers between devices: 4.21 us -> none  [shards(): lax.all_to_all(copies, 'narrow', split_axis=0, concat_axis=0, tiled=True)]
    pallas_call x1 -> x2, Pallas kernels: 6 us -> 6.17 us  [the longest x1 6.09 us: pack(): pl.pallas_call(functools.partial(pack_kernel, owners, peers), out_shape=(...]
  transfers between devices with their start and end apart: 2 -> 1, of which waited for: 2 -> 0; matrix products, arithmetic and copies ran while one was open for 0% -> 0% of each run, Pallas kernels for 3% -> 3%
where the time goes in v5:
time: 78.1 us; the launch traced here: 77.7 us
  blocking collectives  61.8 us (79%)
  Pallas kernels  11.9 us (15%)
  starting transfers between devices  2.91 us (4%)
  loops' own time  0.84 us (1%)
    all_to_all x1, blocking collectives, shards(): lax.all_to_all(sent.reshape(owners, BLOCK, width), 'wide', split_axis=0,...  37.8 us
    all_to_all x1, blocking collectives, shards(): lax.all_to_all(best.reshape(owners, 1, LANES), 'wide', split_axis=0, conc...  13.6 us
    all_to_all x1, blocking collectives, shards(): lax.all_to_all(copies, 'narrow', split_axis=0, concat_axis=0, tiled=True)  10.5 us
    pallas_call x1, Pallas kernels, pack(): pl.pallas_call(functools.partial(pack_kernel, owners, peers), out_shape=(...  6.09 us
    ppermute x1, starting transfers between devices, score(): other = lax.ppermute(rows, 'narrow', [(n, n ^ 1) for n in range(peers)])  2.91 us
    pallas_call x1, Pallas kernels, score(): pl.pallas_call(functools.partial(other_kernel, owners), out_shape=jax.Sha...  1.65 us
    pallas_call x1, Pallas kernels, score(): pl.pallas_call(functools.partial(own_kernel, owners), out_shape=(square,...  1.6 us
  transfers between devices with their start and end apart: 1, of which 0 were waited for; matrix products, arithmetic and copies ran while one was open for 0% of the time, Pallas kernels for 3%

profile of v5, /device:TPU:1, one launch (start us, length us, event | category | flops | bytes accessed | tf_op | source)
XLA Modules:
  0.0 77.7 jit_solution(1027255232268591856)
XLA Ops:
  0.0 0.0 copy-start
  0.0 0.0 copy-start.1
  0.0 0.0 copy-start.2
  0.0 6.1 %pack.1 = (bf16[1024,512]{1,0:T(8,128)(2,1)S(1)}, s32[32,128]{1,0:T(8,128)S(1)}) custom-call(s32[32,128]{1,0:T(8,128)} %bitcast.84, s32[32,128]{1,0:T(8,128)} %bitcast.96, f32[4096]{0:T(1024)} %scale_hbm.1, f32[4096]{0:T(1024)} %bias_hbm.1, bf16[4096,512]{1,0:T(8,128)(2,1)} %codes_hbm.1), custom_call_target="tpu_custom_call" | custom-call | tf_op jit(solution)/shard_map/pack/pallas_call | solution.py:194
  6.1 37.8 %all_to_all.44 = bf16[32,32,512]{2,1,0:T(8,128)(2,1)S(1)} all-to-all(bf16[32,32,512]{2,1,0:T(8,128)(2,1)S(1)} %bitcast.72), channel_id=1, replica_groups=mesh['wide'=32,'narrow'=8] {'wide'}, dimensions={0} | all-to-all | bytes 2097152 | tf_op jit(solution)/shard_map/all_to_all | solution.py:501
  43.9 2.9 %collective-permute-start = (bf16[1024,512]{1,0:T(8,128)(2,1)S(1)}, bf16[1024,512]{1,0:T(8,128)(2,1)S(1)}, u32[]{:S(2)}, u32[]{:S(2)}) collective-permute-start(bf16[1024,512]{1,0:T(8,128)(2,1)S(1)} %bitcast.69), channel_id=1, source_target_pairs={{0,1},{1,0},{2,3},{3,2},{4,5},{5,4},{6,7},{7,6},{8,9},{9,8},{10,11... | collective-permute-start | bytes 3145736 | tf_op jit(solution)/shard_map/ppermute | solution.py:319
  46.8 1.1 %places.1 = (s32[32,128]{1,0:T(8,128)S(1)}, s32[32,128]{1,0:T(8,128)S(1)}) custom-call(s32[32,128]{1,0:T(8,128)S(1)} %get-tuple-element.195.cluster_ref), custom_call_target="tpu_custom_call" | custom-call | flops 1073741824 | bytes 65536 | tf_op jit(solution)/shard_map/places/pallas_call | solution.py:244
  47.9 1.6 %score_own.1 = (f32[128,128]{1,0:T(8,128)S(1)}, f32[128,128]{1,0:T(8,128)S(1)}) custom-call(bf16[1024,512]{1,0:T(8,128)(2,1)S(1)} %bitcast.70), custom_call_target="tpu_custom_call" | custom-call | flops 1073741824 | bytes 2097152 | tf_op jit(solution)/shard_map/score_own/pallas_call | solution.py:322
  49.5 0.0 collective-permute-done.other_ref
  49.5 1.7 %score_other.1 = f32[32,128]{1,0:T(8,128)S(1)} custom-call(bf16[1024,512]{1,0:T(8,128)(2,1)S(1)} %bitcast.71, bf16[1024,512]{1,0:T(8,128)(2,1)S(1)} %collective-permute-done.other_ref, f32[128,128]{1,0:T(8,128)S(1)} %get-tuple-element.199.query_ref, f32[128,128]{1,0:T(8,128)S(1)} %get-tuple-element.200.best_in), custom_call_target="tpu_custom_call" | custom-call | flops 1073741824 | bytes 2097152 | tf_op jit(solution)/shard_map/score_other/pallas_call | solution.py:334
  51.1 13.6 %all_to_all.45 = f32[32,1,128]{2,1,0:T(1,128)S(1)} all-to-all(f32[32,1,128]{2,1,0:T(1,128)S(1)} %bitcast.75), channel_id=1, replica_groups=mesh['wide'=32,'narrow'=8] {'wide'}, dimensions={0} | all-to-all | bytes 32768 | tf_op jit(solution)/shard_map/all_to_all | solution.py:505
  64.7 0.1 spread.1
  64.8 10.5 %all_to_all.46 = f32[8,8,128]{2,1,0:T(8,128)S(1)} all-to-all(f32[8,8,128]{2,1,0:T(8,128)S(1)} %spread.1), channel_id=1, replica_groups=mesh['wide'=32,'narrow'=8] {'narrow'}, dimensions={0} | all-to-all | bytes 65536 | tf_op jit(solution)/shard_map/all_to_all | solution.py:507
  75.3 1.4 %pick.1 = (f32[32,128]{1,0:T(8,128)}, s32[1,1]{1,0:T(1,128)}) custom-call(f32[64,128]{1,0:T(8,128)S(1)} %bitcast.73, s32[32,128]{1,0:T(8,128)S(1)} %get-tuple-element.201.group_ref, s32[32,128]{1,0:T(8,128)S(1)} %get-tuple-element.202.slot_ref), custom_call_target="tpu_custom_call" | custom-call | tf_op jit(solution)/shard_map/pick/pallas_call | solution.py:394
  76.7 0.0 copy-done
  76.7 0.0 copy-done.1
  76.7 0.0 copy-done.2
  76.7 0.8 %while.21 = (s32[]{:T(128)}, f32[4096]{0:T(1024)}, s32[4096]{0:T(1024)S(1)}, bf16[4096,512]{1,0:T(8,128)(2,1)}, f32[4096]{0:T(1024)S(1)}, /*index=5*/f32[4096]{0:T(1024)S(1)}, s32[4096]{0:T(1024)}) while((s32[]{:T(128)}, f32[4096]{0:T(1024)}, s32[4096]{0:T(1024)S(1)}, bf16[4096,512]{1,0:T(8,128)(2,1)}, f32[4096]{0:T(1024)S(1)}, ...), condition=%region_11.12_spmd, body=%region_0.11_spmd | while | flops 1118893056 | bytes 52520216 | solution.py:510
Async XLA Ops:
  0.0 76.7 %copy-start = (s32[4096]{0:T(1024)S(1)}, s32[4096]{0:T(1024)}, u32[]{:S(2)}) copy-start(s32[4096]{0:T(1024)} %param.12) | copy-start | bytes 49156
  0.0 76.7 %copy-start.1 = (f32[4096]{0:T(1024)S(1)}, f32[4096]{0:T(1024)}, u32[]{:S(2)}) copy-start(f32[4096]{0:T(1024)} %scale_hbm.1) | copy-start | bytes 49156
  0.0 76.7 %copy-start.2 = (f32[4096]{0:T(1024)S(1)}, f32[4096]{0:T(1024)}, u32[]{:S(2)}) copy-start(f32[4096]{0:T(1024)} %bias_hbm.1) | copy-start | bytes 49156
  43.9 5.6 %collective-permute-start = (bf16[1024,512]{1,0:T(8,128)(2,1)S(1)}, bf16[1024,512]{1,0:T(8,128)(2,1)S(1)}, u32[]{:S(2)}, u32[]{:S(2)}) collective-permute-start(bf16[1024,512]{1,0:T(8,128)(2,1)S(1)} %bitcast.69), channel_id=1, source_target_pairs={{0,1},{1,0},{2,3},{3,2},{4,5},{5,4},{6,7},{7,6},{8,9},{9,8},{10,11... | collective-permute-start | bytes 3145736 | tf_op jit(solution)/shard_map/ppermute | solution.py:319

commit v6 on v5

--- a/solution.py
+++ b/solution.py
@@ -150,14 +150,14 @@
     for copy in [table_copy] + small_copies:
         copy.wait()
 
-    def two_owners(half, carry):
-        pair = (2 * half, 2 * half + 1)
-        used = jnp.maximum(table_smem[BLOCK, pair[0]], table_smem[BLOCK, pair[1]])
-
-        def eight_rows(group, carry):
-            for owner in pair:
-                for n in range(8):
-                    slot = group * 8 + n
+    def four_owners(quarter, carry):
+        four = [4 * quarter + n for n in range(4)]
+        used = functools.reduce(jnp.maximum, [table_smem[BLOCK, owner] for owner in four])
+
+        def four_rows(group, carry):
+            for owner in four:
+                for n in range(4):
+                    slot = group * 4 + n
                     row = table_smem[slot, owner]
                     slots_full[pl.ds((owner * BLOCK + slot) * PITCH, TAKE), :] = (
                         codes_full[pl.ds(row * PITCH, TAKE), :] * scale_ref[row]
@@ -165,9 +165,9 @@
                     )
             return carry
 
-        return lax.fori_loop(0, (used + 7) // 8, eight_rows, carry)
-
-    lax.fori_loop(0, owners // 2, two_owners, 0)
+        return lax.fori_loop(0, (used + 3) // 4, four_rows, carry)
+
+    lax.fori_loop(0, owners // 4, four_owners, 0)
 
     pair = 2 * BLOCK
     width = tiles * LANES
@@ -201,8 +201,8 @@
         out_specs=(whole, whole),
         scratch_shapes=[
             pltpu.VMEM((local_rows, width), jnp.bfloat16),
-            pltpu.VMEM((local_rows * PITCH, LANES), jnp.float32),
-            pltpu.VMEM((owners * BLOCK * PITCH, LANES), jnp.float32),
+            pltpu.VMEM((local_rows * PITCH + 8, LANES), jnp.float32),
+            pltpu.VMEM((owners * BLOCK * PITCH + 8, LANES), jnp.float32),
             pltpu.VMEM((BLOCK + 8, LANES), jnp.int32),
             pltpu.SMEM((BLOCK + 8, LANES), jnp.int32),
             pltpu.SMEM((local_rows,), jnp.float32),

time: 78.1 us -> 77.9 us (level)
  no operation moved by 1% of the time
where the time goes in v6:
time: 77.9 us; the launch traced here: 77.6 us
  blocking collectives  62 us (80%)
  Pallas kernels  11.6 us (15%)
  starting transfers between devices  2.91 us (4%)
  loops' own time  0.84 us (1%)
    all_to_all x1, blocking collectives, shards(): lax.all_to_all(sent.reshape(owners, BLOCK, width), 'wide', split_axis=0,...  37.9 us
    all_to_all x1, blocking collectives, shards(): lax.all_to_all(best.reshape(owners, 1, LANES), 'wide', split_axis=0, conc...  13.6 us
    all_to_all x1, blocking collectives, shards(): lax.all_to_all(copies, 'narrow', split_axis=0, concat_axis=0, tiled=True)  10.5 us
    pallas_call x1, Pallas kernels, pack(): pl.pallas_call(functools.partial(pack_kernel, owners, peers), out_shape=(...  5.79 us
    ppermute x1, starting transfers between devices, score(): other = lax.ppermute(rows, 'narrow', [(n, n ^ 1) for n in range(peers)])  2.91 us
    pallas_call x1, Pallas kernels, score(): pl.pallas_call(functools.partial(other_kernel, owners), out_shape=jax.Sha...  1.65 us
    pallas_call x1, Pallas kernels, score(): pl.pallas_call(functools.partial(own_kernel, owners), out_shape=(square,...  1.6 us
  transfers between devices with their start and end apart: 1, of which 0 were waited for; matrix products, arithmetic and copies ran while one was open for 0% of the time, Pallas kernels for 3%

profile of v6, /device:TPU:1, one launch (start us, length us, event | category | flops | bytes accessed | tf_op | source)
XLA Modules:
  0.0 77.6 jit_solution(17065391700925251833)
XLA Ops:
  0.0 0.0 copy-start
  0.0 0.0 copy-start.1
  0.0 0.0 copy-start.2
  0.0 5.8 %pack.1 = (bf16[1024,512]{1,0:T(8,128)(2,1)S(1)}, s32[32,128]{1,0:T(8,128)S(1)}) custom-call(s32[32,128]{1,0:T(8,128)} %bitcast.84, s32[32,128]{1,0:T(8,128)} %bitcast.96, f32[4096]{0:T(1024)} %scale_hbm.1, f32[4096]{0:T(1024)} %bias_hbm.1, bf16[4096,512]{1,0:T(8,128)(2,1)} %codes_hbm.1), custom_call_target="tpu_custom_call" | custom-call | tf_op jit(solution)/shard_map/pack/pallas_call | solution.py:194
  5.8 37.9 %all_to_all.44 = bf16[32,32,512]{2,1,0:T(8,128)(2,1)S(1)} all-to-all(bf16[32,32,512]{2,1,0:T(8,128)(2,1)S(1)} %bitcast.72), channel_id=1, replica_groups=mesh['wide'=32,'narrow'=8] {'wide'}, dimensions={0} | all-to-all | bytes 2097152 | tf_op jit(solution)/shard_map/all_to_all | solution.py:501
  43.7 2.9 %collective-permute-start = (bf16[1024,512]{1,0:T(8,128)(2,1)S(1)}, bf16[1024,512]{1,0:T(8,128)(2,1)S(1)}, u32[]{:S(2)}, u32[]{:S(2)}) collective-permute-start(bf16[1024,512]{1,0:T(8,128)(2,1)S(1)} %bitcast.69), channel_id=1, source_target_pairs={{0,1},{1,0},{2,3},{3,2},{4,5},{5,4},{6,7},{7,6},{8,9},{9,8},{10,11... | collective-permute-start | bytes 3145736 | tf_op jit(solution)/shard_map/ppermute | solution.py:319
  46.6 1.1 %places.1 = (s32[32,128]{1,0:T(8,128)S(1)}, s32[32,128]{1,0:T(8,128)S(1)}) custom-call(s32[32,128]{1,0:T(8,128)S(1)} %get-tuple-element.195.cluster_ref), custom_call_target="tpu_custom_call" | custom-call | flops 1073741824 | bytes 65536 | tf_op jit(solution)/shard_map/places/pallas_call | solution.py:244
  47.7 1.6 %score_own.1 = (f32[128,128]{1,0:T(8,128)S(1)}, f32[128,128]{1,0:T(8,128)S(1)}) custom-call(bf16[1024,512]{1,0:T(8,128)(2,1)S(1)} %bitcast.70), custom_call_target="tpu_custom_call" | custom-call | flops 1073741824 | bytes 2097152 | tf_op jit(solution)/shard_map/score_own/pallas_call | solution.py:322
  49.3 0.0 collective-permute-done.other_ref
  49.3 1.7 %score_other.1 = f32[32,128]{1,0:T(8,128)S(1)} custom-call(bf16[1024,512]{1,0:T(8,128)(2,1)S(1)} %bitcast.71, bf16[1024,512]{1,0:T(8,128)(2,1)S(1)} %collective-permute-done.other_ref, f32[128,128]{1,0:T(8,128)S(1)} %get-tuple-element.199.query_ref, f32[128,128]{1,0:T(8,128)S(1)} %get-tuple-element.200.best_in), custom_call_target="tpu_custom_call" | custom-call | flops 1073741824 | bytes 2097152 | tf_op jit(solution)/shard_map/score_other/pallas_call | solution.py:334
  51.0 13.6 %all_to_all.45 = f32[32,1,128]{2,1,0:T(1,128)S(1)} all-to-all(f32[32,1,128]{2,1,0:T(1,128)S(1)} %bitcast.75), channel_id=1, replica_groups=mesh['wide'=32,'narrow'=8] {'wide'}, dimensions={0} | all-to-all | bytes 32768 | tf_op jit(solution)/shard_map/all_to_all | solution.py:505
  64.6 0.1 spread.1
  64.6 10.5 %all_to_all.46 = f32[8,8,128]{2,1,0:T(8,128)S(1)} all-to-all(f32[8,8,128]{2,1,0:T(8,128)S(1)} %spread.1), channel_id=1, replica_groups=mesh['wide'=32,'narrow'=8] {'narrow'}, dimensions={0} | all-to-all | bytes 65536 | tf_op jit(solution)/shard_map/all_to_all | solution.py:507
  75.1 1.4 %pick.1 = (f32[32,128]{1,0:T(8,128)}, s32[1,1]{1,0:T(1,128)}) custom-call(f32[64,128]{1,0:T(8,128)S(1)} %bitcast.73, s32[32,128]{1,0:T(8,128)S(1)} %get-tuple-element.201.group_ref, s32[32,128]{1,0:T(8,128)S(1)} %get-tuple-element.202.slot_ref), custom_call_target="tpu_custom_call" | custom-call | tf_op jit(solution)/shard_map/pick/pallas_call | solution.py:394
  76.5 0.0 copy-done
  76.5 0.0 copy-done.1
  76.5 0.0 copy-done.2
  76.6 0.8 %while.21 = (s32[]{:T(128)}, f32[4096]{0:T(1024)}, s32[4096]{0:T(1024)S(1)}, bf16[4096,512]{1,0:T(8,128)(2,1)}, f32[4096]{0:T(1024)S(1)}, /*index=5*/f32[4096]{0:T(1024)S(1)}, s32[4096]{0:T(1024)}) while((s32[]{:T(128)}, f32[4096]{0:T(1024)}, s32[4096]{0:T(1024)S(1)}, bf16[4096,512]{1,0:T(8,128)(2,1)}, f32[4096]{0:T(1024)S(1)}, ...), condition=%region_11.12_spmd, body=%region_0.11_spmd | while | flops 1118893056 | bytes 52520216 | solution.py:510
Async XLA Ops:
  0.0 76.5 %copy-start = (s32[4096]{0:T(1024)S(1)}, s32[4096]{0:T(1024)}, u32[]{:S(2)}) copy-start(s32[4096]{0:T(1024)} %param.12) | copy-start | bytes 49156
  0.0 76.5 %copy-start.1 = (f32[4096]{0:T(1024)S(1)}, f32[4096]{0:T(1024)}, u32[]{:S(2)}) copy-start(f32[4096]{0:T(1024)} %scale_hbm.1) | copy-start | bytes 49156
  0.0 76.5 %copy-start.2 = (f32[4096]{0:T(1024)S(1)}, f32[4096]{0:T(1024)}, u32[]{:S(2)}) copy-start(f32[4096]{0:T(1024)} %bias_hbm.1) | copy-start | bytes 49156
  43.7 5.6 %collective-permute-start = (bf16[1024,512]{1,0:T(8,128)(2,1)S(1)}, bf16[1024,512]{1,0:T(8,128)(2,1)S(1)}, u32[]{:S(2)}, u32[]{:S(2)}) collective-permute-start(bf16[1024,512]{1,0:T(8,128)(2,1)S(1)} %bitcast.69), channel_id=1, source_target_pairs={{0,1},{1,0},{2,3},{3,2},{4,5},{5,4},{6,7},{7,6},{8,9},{9,8},{10,11... | collective-permute-start | bytes 3145736 | tf_op jit(solution)/shard_map/ppermute | solution.py:319

commit v7 on v6

--- a/solution.py
+++ b/solution.py
@@ -379,12 +379,17 @@
     middle = rest.astype(jnp.bfloat16)
     low = (rest - middle.astype(jnp.float32)).astype(jnp.bfloat16)
     parts = jnp.concatenate([high, middle, low], axis=0)
-    for n in range(group_ref.shape[0] // 2):
-        one_hot = jnp.where(iota((groups, CHUNK), 0) == chunk_of(group_ref, n), 1.0, 0.0).astype(jnp.bfloat16)
-        by_slot = dot(parts, one_hot, 1, 0)
-        by_slot = by_slot[:BLOCK] + by_slot[BLOCK : 2 * BLOCK] + by_slot[2 * BLOCK :]
+    chunks = group_ref.shape[0] // 2
+    hots = [
+        jnp.where(iota((groups, CHUNK), 0) == chunk_of(group_ref, n), 1.0, 0.0).astype(jnp.bfloat16)
+        for n in range(chunks)
+    ]
+    by_slot = dot(parts, jnp.concatenate(hots, axis=1), 1, 0)
+    by_slot = by_slot[:BLOCK] + by_slot[BLOCK : 2 * BLOCK] + by_slot[2 * BLOCK :]
+    for n in range(chunks):
         here = iota((BLOCK, CHUNK), 0) == chunk_of(slot_ref, n)
-        picked = jnp.sum(jnp.where(here, by_slot, 0.0), axis=0, keepdims=True)
+        mine = by_slot[:, n * CHUNK : (n + 1) * CHUNK]
+        picked = jnp.sum(jnp.where(here, mine, 0.0), axis=0, keepdims=True)
         out_ref[2 * n : 2 * n + 1, :] = picked[:, :LANES]
         out_ref[2 * n + 1 : 2 * n + 2, :] = picked[:, LANES:]
 

time: 77.9 us -> 77.9 us (level)
  no operation moved by 1% of the time
where the time goes in v7:
time: 77.9 us; the launch traced here: 77.6 us
  blocking collectives  61.9 us (79%)
  Pallas kernels  11.5 us (15%)
  starting transfers between devices  3.07 us (4%)
  loops' own time  0.84 us (1%)
    all_to_all x1, blocking collectives, shards(): lax.all_to_all(sent.reshape(owners, BLOCK, width), 'wide', split_axis=0,...  37.9 us
    all_to_all x1, blocking collectives, shards(): lax.all_to_all(best.reshape(owners, 1, LANES), 'wide', split_axis=0, conc...  13.6 us
    all_to_all x1, blocking collectives, shards(): lax.all_to_all(copies, 'narrow', split_axis=0, concat_axis=0, tiled=True)  10.5 us
    pallas_call x1, Pallas kernels, pack(): pl.pallas_call(functools.partial(pack_kernel, owners, peers), out_shape=(...  5.74 us
    ppermute x1, starting transfers between devices, score(): other = lax.ppermute(rows, 'narrow', [(n, n ^ 1) for n in range(peers)])  3.07 us
    pallas_call x1, Pallas kernels, score(): pl.pallas_call(functools.partial(other_kernel, owners), out_shape=jax.Sha...  1.65 us
    pallas_call x1, Pallas kernels, score(): pl.pallas_call(functools.partial(own_kernel, owners), out_shape=(square,...  1.61 us
  transfers between devices with their start and end apart: 1, of which 0 were waited for; matrix products, arithmetic and copies ran while one was open for 0% of the time, Pallas kernels for 3%

profile of v7, /device:TPU:1, one launch (start us, length us, event | category | flops | bytes accessed | tf_op | source)
XLA Modules:
  0.0 77.6 jit_solution(17065391700925251833)
XLA Ops:
  0.0 0.0 copy-start
  0.0 0.0 copy-start.1
  0.0 0.0 copy-start.2
  0.0 5.7 %pack.1 = (bf16[1024,512]{1,0:T(8,128)(2,1)S(1)}, s32[32,128]{1,0:T(8,128)S(1)}) custom-call(s32[32,128]{1,0:T(8,128)} %bitcast.84, s32[32,128]{1,0:T(8,128)} %bitcast.96, f32[4096]{0:T(1024)} %scale_hbm.1, f32[4096]{0:T(1024)} %bias_hbm.1, bf16[4096,512]{1,0:T(8,128)(2,1)} %codes_hbm.1), custom_call_target="tpu_custom_call" | custom-call | tf_op jit(solution)/shard_map/pack/pallas_call | solution.py:194
  5.8 37.9 %all_to_all.44 = bf16[32,32,512]{2,1,0:T(8,128)(2,1)S(1)} all-to-all(bf16[32,32,512]{2,1,0:T(8,128)(2,1)S(1)} %bitcast.72), channel_id=1, replica_groups=mesh['wide'=32,'narrow'=8] {'wide'}, dimensions={0} | all-to-all | bytes 2097152 | tf_op jit(solution)/shard_map/all_to_all | solution.py:506
  43.6 3.1 %collective-permute-start = (bf16[1024,512]{1,0:T(8,128)(2,1)S(1)}, bf16[1024,512]{1,0:T(8,128)(2,1)S(1)}, u32[]{:S(2)}, u32[]{:S(2)}) collective-permute-start(bf16[1024,512]{1,0:T(8,128)(2,1)S(1)} %bitcast.69), channel_id=1, source_target_pairs={{0,1},{1,0},{2,3},{3,2},{4,5},{5,4},{6,7},{7,6},{8,9},{9,8},{10,11... | collective-permute-start | bytes 3145736 | tf_op jit(solution)/shard_map/ppermute | solution.py:319
  46.7 1.1 %places.1 = (s32[32,128]{1,0:T(8,128)S(1)}, s32[32,128]{1,0:T(8,128)S(1)}) custom-call(s32[32,128]{1,0:T(8,128)S(1)} %get-tuple-element.195.cluster_ref), custom_call_target="tpu_custom_call" | custom-call | flops 1073741824 | bytes 65536 | tf_op jit(solution)/shard_map/places/pallas_call | solution.py:244
  47.8 1.6 %score_own.1 = (f32[128,128]{1,0:T(8,128)S(1)}, f32[128,128]{1,0:T(8,128)S(1)}) custom-call(bf16[1024,512]{1,0:T(8,128)(2,1)S(1)} %bitcast.70), custom_call_target="tpu_custom_call" | custom-call | flops 1073741824 | bytes 2097152 | tf_op jit(solution)/shard_map/score_own/pallas_call | solution.py:322
  49.4 0.0 collective-permute-done.other_ref
  49.4 1.6 %score_other.1 = f32[32,128]{1,0:T(8,128)S(1)} custom-call(bf16[1024,512]{1,0:T(8,128)(2,1)S(1)} %bitcast.71, bf16[1024,512]{1,0:T(8,128)(2,1)S(1)} %collective-permute-done.other_ref, f32[128,128]{1,0:T(8,128)S(1)} %get-tuple-element.199.query_ref, f32[128,128]{1,0:T(8,128)S(1)} %get-tuple-element.200.best_in), custom_call_target="tpu_custom_call" | custom-call | flops 1073741824 | bytes 2097152 | tf_op jit(solution)/shard_map/score_other/pallas_call | solution.py:334
  51.1 13.6 %all_to_all.45 = f32[32,1,128]{2,1,0:T(1,128)S(1)} all-to-all(f32[32,1,128]{2,1,0:T(1,128)S(1)} %bitcast.75), channel_id=1, replica_groups=mesh['wide'=32,'narrow'=8] {'wide'}, dimensions={0} | all-to-all | bytes 32768 | tf_op jit(solution)/shard_map/all_to_all | solution.py:510
  64.6 0.1 spread.1
  64.7 10.5 %all_to_all.46 = f32[8,8,128]{2,1,0:T(8,128)S(1)} all-to-all(f32[8,8,128]{2,1,0:T(8,128)S(1)} %spread.1), channel_id=1, replica_groups=mesh['wide'=32,'narrow'=8] {'narrow'}, dimensions={0} | all-to-all | bytes 65536 | tf_op jit(solution)/shard_map/all_to_all | solution.py:512
  75.1 1.4 %pick.1 = (f32[32,128]{1,0:T(8,128)}, s32[1,1]{1,0:T(1,128)}) custom-call(f32[64,128]{1,0:T(8,128)S(1)} %bitcast.73, s32[32,128]{1,0:T(8,128)S(1)} %get-tuple-element.201.group_ref, s32[32,128]{1,0:T(8,128)S(1)} %get-tuple-element.202.slot_ref), custom_call_target="tpu_custom_call" | custom-call | tf_op jit(solution)/shard_map/pick/pallas_call | solution.py:399
  76.5 0.0 copy-done
  76.5 0.0 copy-done.1
  76.5 0.0 copy-done.2
  76.6 0.8 %while.21 = (s32[]{:T(128)}, f32[4096]{0:T(1024)}, s32[4096]{0:T(1024)S(1)}, bf16[4096,512]{1,0:T(8,128)(2,1)}, f32[4096]{0:T(1024)S(1)}, /*index=5*/f32[4096]{0:T(1024)S(1)}, s32[4096]{0:T(1024)}) while((s32[]{:T(128)}, f32[4096]{0:T(1024)}, s32[4096]{0:T(1024)S(1)}, bf16[4096,512]{1,0:T(8,128)(2,1)}, f32[4096]{0:T(1024)S(1)}, ...), condition=%region_11.12_spmd, body=%region_0.11_spmd | while | flops 1118893056 | bytes 52520216 | solution.py:515
Async XLA Ops:
  0.0 76.5 %copy-start = (s32[4096]{0:T(1024)S(1)}, s32[4096]{0:T(1024)}, u32[]{:S(2)}) copy-start(s32[4096]{0:T(1024)} %param.12) | copy-start | bytes 49156
  0.0 76.5 %copy-start.1 = (f32[4096]{0:T(1024)S(1)}, f32[4096]{0:T(1024)}, u32[]{:S(2)}) copy-start(f32[4096]{0:T(1024)} %scale_hbm.1) | copy-start | bytes 49156
  0.0 76.5 %copy-start.2 = (f32[4096]{0:T(1024)S(1)}, f32[4096]{0:T(1024)}, u32[]{:S(2)}) copy-start(f32[4096]{0:T(1024)} %bias_hbm.1) | copy-start | bytes 49156
  43.6 5.8 %collective-permute-start = (bf16[1024,512]{1,0:T(8,128)(2,1)S(1)}, bf16[1024,512]{1,0:T(8,128)(2,1)S(1)}, u32[]{:S(2)}, u32[]{:S(2)}) collective-permute-start(bf16[1024,512]{1,0:T(8,128)(2,1)S(1)} %bitcast.69), channel_id=1, source_target_pairs={{0,1},{1,0},{2,3},{3,2},{4,5},{5,4},{6,7},{7,6},{8,9},{9,8},{10,11... | collective-permute-start | bytes 3145736 | tf_op jit(solution)/shard_map/ppermute | solution.py:319
